TPU v7x, 32 devices: a whole 2x2x4 slice. The times are simulated.
32 devices in a mesh: dp: 8 (over y, x, core), seq: 4 (over z).
Axes of the slice: x: 2, y: 2, z: 4, core: 2. Of those that a mesh axis runs over, the one named last changes fastest.
Arguments:
- inputs: bfloat16 [16, 16, 256, 768], P('dp', 'seq'), may hold values from -6 to 6
- norm_one_gain: bfloat16 [768], P(('dp', 'seq')), may hold values from 0.25 to 1.75
- norm_one_shift: bfloat16 [768], P(('dp', 'seq')), may hold values from -2 to 2
- space_qkv: bfloat16 [768, 2304], P(('dp', 'seq')), may hold values from -0.21875 to 0.21875
- space_qv_bias: bfloat16 [1536], P(('dp', 'seq')), may hold values from -2 to 2
- space_out: bfloat16 [768, 768], P(('dp', 'seq')), may hold values from -0.875 to 0.875
- space_out_bias: bfloat16 [768], P(('dp', 'seq')), may hold values from -2 to 2
- norm_two_gain: bfloat16 [768], P(('dp', 'seq')), may hold values from 0.25 to 1.75
- norm_two_shift: bfloat16 [768], P(('dp', 'seq')), may hold values from -2 to 2
- time_qkv: bfloat16 [768, 2304], P(('dp', 'seq')), may hold values from -0.21875 to 0.21875
- time_qv_bias: bfloat16 [1536], P(('dp', 'seq')), may hold values from -2 to 2
- time_out: bfloat16 [768, 768], P(('dp', 'seq')), may hold values from -0.4375 to 0.4375
- time_out_bias: bfloat16 [768], P(('dp', 'seq')), may hold values from -2 to 2
- norm_three_gain: bfloat16 [768], P(('dp', 'seq')), may hold values from 0.25 to 1.75
- norm_three_shift: bfloat16 [768], P(('dp', 'seq')), may hold values from -2 to 2
- mlp_in: bfloat16 [768, 3072], P(('dp', 'seq')), may hold values from -0.21875 to 0.21875
- mlp_in_bias: bfloat16 [3072], P(('dp', 'seq')), may hold values from -2 to 2
- mlp_out: bfloat16 [3072, 768], P(('dp', 'seq')), may hold values from -0.109375 to 0.109375
- mlp_out_bias: bfloat16 [768], P(('dp', 'seq')), may hold values from -2 to 2
- cotangent: bfloat16 [16, 16, 256, 768], P('dp', 'seq'), may hold values from -6 to 6
Outputs:
- output: bfloat16 [16, 16, 256, 768], P('dp', 'seq')
- grad_inputs: bfloat16 [16, 16, 256, 768], P('dp', 'seq')
- grad_norm_one_gain: float32 [768], P(('dp', 'seq'))
- grad_norm_one_shift: float32 [768], P(('dp', 'seq'))
- grad_space_qkv: float32 [768, 2304], P(('dp', 'seq'))
- grad_space_qv_bias: float32 [1536], P(('dp', 'seq'))
- grad_space_out: float32 [768, 768], P(('dp', 'seq'))
- grad_space_out_bias: float32 [768], P(('dp', 'seq'))
- grad_norm_two_gain: float32 [768], P(('dp', 'seq'))
- grad_norm_two_shift: float32 [768], P(('dp', 'seq'))
- grad_time_qkv: float32 [768, 2304], P(('dp', 'seq'))
- grad_time_qv_bias: float32 [1536], P(('dp', 'seq'))
- grad_time_out: float32 [768, 768], P(('dp', 'seq'))
- grad_time_out_bias: float32 [768], P(('dp', 'seq'))
- grad_norm_three_gain: float32 [768], P(('dp', 'seq'))
- grad_norm_three_shift: float32 [768], P(('dp', 'seq'))
- grad_mlp_in: float32 [768, 3072], P(('dp', 'seq'))
- grad_mlp_in_bias: float32 [3072], P(('dp', 'seq'))
- grad_mlp_out: float32 [3072, 768], P(('dp', 'seq'))
- grad_mlp_out_bias: float32 [768], P(('dp', 'seq'))
All inputs are finite; a program needn't handle non-finite values.
Results may differ from a plain program's by a relative error of at most 0.023.
Values may be sent and summed in bfloat16 or wider, within the bound.
A program may use at most 448 MiB of HBM per device.

v0:
```python
import jax
import jax.numpy as jnp
from jax import lax
from jax.sharding import PartitionSpec as P

HEADS = 12
HD = 64
MICRO = 2


EPS = 1e-06
SCALE = 0.125


def as_sent(x):

    def short(part):
        return part.astype(jnp.bfloat16) if part.dtype == jnp.float32 else part

    return jax.tree.map(short, x)


def wide(value):
    return value.astype(jnp.float32)


def outer_sum(left, right):
    return lax.dot_general(
        left, right, (((0,), (0,)), ((), ())), preferred_element_type=jnp.float32
    )


def back_dot(grad, weight):
    return lax.dot_general(
        grad, weight, (((1,), (1,)), ((), ())), preferred_element_type=jnp.float32
    )


def gelu_exact(value):
    return jax.nn.gelu(value, approximate=False)


def norm_fwd(rows, gain, shift):
    center = rows - jnp.mean(rows, axis=-1, keepdims=True)
    rstd_val = lax.rsqrt(jnp.mean(center * center, axis=-1, keepdims=True) + EPS)
    normal = center * rstd_val
    return (normal * gain + shift, normal, rstd_val)


def norm_back(grad, normal, rstd_val, gain):
    grad_gain = jnp.sum(grad * normal, axis=0)
    grad_shift = jnp.sum(grad, axis=0)
    scaled = grad * gain
    inner = (
        scaled
        - jnp.mean(scaled, axis=-1, keepdims=True)
        - normal * jnp.mean(scaled * normal, axis=-1, keepdims=True)
    )
    return (rstd_val * inner, grad_gain, grad_shift)


def attend(rows, seq_count, w_qkv, b_qv, w_out, b_out):
    width = w_out.shape[0]
    length = rows.shape[0] // seq_count
    bias = jnp.concatenate([b_qv[:width], jnp.zeros((width,), jnp.float32), b_qv[width:]])
    project = (jnp.dot(rows, w_qkv, preferred_element_type=jnp.float32) + bias).astype(jnp.bfloat16)
    project = project.reshape(seq_count, length, 3, HEADS, HD)
    query, keys, values = (project[:, :, 0], project[:, :, 1], project[:, :, 2])
    scores = jnp.einsum("blhd,bmhd->bhlm", query, keys, preferred_element_type=jnp.float32) * SCALE
    lse_top = jax.nn.logsumexp(scores, axis=-1, keepdims=True)
    weights = jnp.exp(scores - lse_top).astype(jnp.bfloat16)
    mixed = jnp.einsum("bhlm,bmhd->blhd", weights, values, preferred_element_type=jnp.float32)
    mixed = mixed.astype(jnp.bfloat16).reshape(seq_count * length, width)
    branch = jnp.dot(mixed, w_out, preferred_element_type=jnp.float32) + b_out
    return (branch, (query, keys, values, lse_top, mixed))


def attend_back(rows, grad_rows, kept, w_qkv, w_out):
    query, keys, values, lse_top, mixed = kept
    seq_count, length = (query.shape[0], query.shape[1])
    width = w_out.shape[0]
    grad_out_w = outer_sum(mixed, grad_rows)
    grad_out_b = jnp.sum(wide(grad_rows), axis=0)
    grad_mixed = (
        back_dot(grad_rows, w_out).astype(jnp.bfloat16).reshape(seq_count, length, HEADS, HD)
    )
    scores = jnp.einsum("blhd,bmhd->bhlm", query, keys, preferred_element_type=jnp.float32) * SCALE
    probs = jnp.exp(scores - lse_top)
    grad_values = jnp.einsum(
        "bhlm,blhd->bmhd",
        probs.astype(jnp.bfloat16),
        grad_mixed,
        preferred_element_type=jnp.float32,
    )
    grad_probs = jnp.einsum(
        "blhd,bmhd->bhlm", grad_mixed, values, preferred_element_type=jnp.float32
    )
    delta_row = jnp.sum(probs * grad_probs, axis=-1, keepdims=True)
    grad_scores = (probs * (grad_probs - delta_row)).astype(jnp.bfloat16)
    grad_query = (
        jnp.einsum("bhlm,bmhd->blhd", grad_scores, keys, preferred_element_type=jnp.float32) * SCALE
    )
    grad_keys = (
        jnp.einsum("bhlm,blhd->bmhd", grad_scores, query, preferred_element_type=jnp.float32)
        * SCALE
    )
    grad_proj = jnp.stack([grad_query, grad_keys, grad_values], axis=2).astype(jnp.bfloat16)
    grad_proj = grad_proj.reshape(seq_count * length, 3 * width)
    grad_qkv_w = outer_sum(rows, grad_proj)
    column_sums = jnp.sum(wide(grad_proj), axis=0)
    grad_qv_b = jnp.concatenate([column_sums[:width], column_sums[2 * width :]])
    grad_rows_in = back_dot(grad_proj, w_qkv)
    return (grad_rows_in, (grad_qkv_w, grad_qv_b, grad_out_w, grad_out_b))


def forward(block, full):
    (
        gain_one,
        shift_one,
        space_qkv,
        space_bias,
        space_out,
        space_out_b,
        gain_two,
        shift_two,
        time_qkv,
        time_bias,
        time_out,
        time_out_b,
        gain_three,
        shift_three,
        mlp_in,
        mlp_in_b,
        mlp_out,
        mlp_out_b,
    ) = full
    clip_count, frame_count, place_count, width = block.shape
    resid_zero = wide(block).reshape(-1, width)
    normed, normal_one, rstd_one = norm_fwd(resid_zero, wide(gain_one), wide(shift_one))
    space_rows = normed.astype(jnp.bfloat16)
    branch, space_kept = attend(
        space_rows,
        clip_count * frame_count,
        space_qkv,
        wide(space_bias),
        space_out,
        wide(space_out_b),
    )
    resid_one = resid_zero + branch
    normed, normal_two, rstd_two = norm_fwd(resid_one, wide(gain_two), wide(shift_two))
    by_frame = normed.astype(jnp.bfloat16).reshape(clip_count, frame_count, place_count, width)
    by_place = lax.all_to_all(by_frame, "seq", split_axis=2, concat_axis=1, tiled=True)
    all_frames, own_places = (by_place.shape[1], by_place.shape[2])
    time_rows = jnp.transpose(by_place, (0, 2, 1, 3)).reshape(-1, width)
    branch, time_kept = attend(
        time_rows, clip_count * own_places, time_qkv, wide(time_bias), time_out, wide(time_out_b)
    )
    branch = branch.astype(jnp.bfloat16).reshape(clip_count, own_places, all_frames, width)
    branch = lax.all_to_all(
        jnp.transpose(branch, (0, 2, 1, 3)), "seq", split_axis=1, concat_axis=2, tiled=True
    )
    resid_two = resid_one + wide(branch).reshape(-1, width)
    normed, normal_three, rstd_three = norm_fwd(resid_two, wide(gain_three), wide(shift_three))
    mlp_rows = normed.astype(jnp.bfloat16)
    hidden = jnp.dot(mlp_rows, mlp_in, preferred_element_type=jnp.float32) + wide(mlp_in_b)
    active = gelu_exact(hidden).astype(jnp.bfloat16)
    result = resid_two + (
        jnp.dot(active, mlp_out, preferred_element_type=jnp.float32) + wide(mlp_out_b)
    )
    saved = (
        space_rows,
        normal_one,
        rstd_one,
        space_kept,
        time_rows,
        normal_two,
        rstd_two,
        time_kept,
        mlp_rows,
        normal_three,
        rstd_three,
        hidden,
        active,
    )
    return (result.astype(jnp.bfloat16).reshape(block.shape), saved)


def backward(saved, grad_block, full):
    (
        gain_one,
        shift_one,
        space_qkv,
        space_bias,
        space_out,
        space_out_b,
        gain_two,
        shift_two,
        time_qkv,
        time_bias,
        time_out,
        time_out_b,
        gain_three,
        shift_three,
        mlp_in,
        mlp_in_b,
        mlp_out,
        mlp_out_b,
    ) = full
    (
        space_rows,
        normal_one,
        rstd_one,
        space_kept,
        time_rows,
        normal_two,
        rstd_two,
        time_kept,
        mlp_rows,
        normal_three,
        rstd_three,
        hidden,
        active,
    ) = saved
    clip_count, frame_count, place_count, width = grad_block.shape
    grad_top = grad_block.reshape(-1, width)
    grad_mlp_out = outer_sum(active, grad_top)
    grad_mlp_out_b = jnp.sum(wide(grad_top), axis=0)
    grad_active = back_dot(grad_top, mlp_out)
    pull_back = jax.vjp(gelu_exact, hidden)[1]
    grad_hidden = pull_back(grad_active)[0].astype(jnp.bfloat16)
    grad_mlp_in = outer_sum(mlp_rows, grad_hidden)
    grad_mlp_in_b = jnp.sum(wide(grad_hidden), axis=0)
    grad_normed = back_dot(grad_hidden, mlp_in)
    grad_rows, grad_gain_three, grad_shift_three = norm_back(
        grad_normed, normal_three, rstd_three, wide(gain_three)
    )
    grad_two = wide(grad_top) + grad_rows
    sent = grad_two.astype(jnp.bfloat16).reshape(grad_block.shape)
    by_place = lax.all_to_all(sent, "seq", split_axis=2, concat_axis=1, tiled=True)
    all_frames, own_places = (by_place.shape[1], by_place.shape[2])
    grad_time = jnp.transpose(by_place, (0, 2, 1, 3)).reshape(-1, width)
    grad_normed, time_terms = attend_back(time_rows, grad_time, time_kept, time_qkv, time_out)
    grad_normed = grad_normed.astype(jnp.bfloat16).reshape(
        clip_count, own_places, all_frames, width
    )
    grad_normed = lax.all_to_all(
        jnp.transpose(grad_normed, (0, 2, 1, 3)), "seq", split_axis=1, concat_axis=2, tiled=True
    )
    grad_rows, grad_gain_two, grad_shift_two = norm_back(
        wide(grad_normed).reshape(-1, width), normal_two, rstd_two, wide(gain_two)
    )
    grad_one = grad_two + grad_rows
    grad_normed, space_terms = attend_back(
        space_rows, grad_one.astype(jnp.bfloat16), space_kept, space_qkv, space_out
    )
    grad_rows, grad_gain_one, grad_shift_one = norm_back(
        grad_normed, normal_one, rstd_one, wide(gain_one)
    )
    grad_zero = grad_one + grad_rows
    terms = (
        (grad_gain_one, grad_shift_one)
        + space_terms
        + (grad_gain_two, grad_shift_two)
        + time_terms
        + (
            grad_gain_three,
            grad_shift_three,
            grad_mlp_in,
            grad_mlp_in_b,
            grad_mlp_out,
            grad_mlp_out_b,
        )
    )
    return (grad_zero.astype(jnp.bfloat16).reshape(grad_block.shape), terms)


def add_terms(total, terms):
    if total is None:
        return terms
    return tuple((left + right for left, right in zip(total, terms)))


def on_device(
    inputs,
    norm_one_gain,
    norm_one_shift,
    space_qkv,
    space_qv_bias,
    space_out,
    space_out_bias,
    norm_two_gain,
    norm_two_shift,
    time_qkv,
    time_qv_bias,
    time_out,
    time_out_bias,
    norm_three_gain,
    norm_three_shift,
    mlp_in,
    mlp_in_bias,
    mlp_out,
    mlp_out_bias,
    cotangent,
):
    shards = (
        norm_one_gain,
        norm_one_shift,
        space_qkv,
        space_qv_bias,
        space_out,
        space_out_bias,
        norm_two_gain,
        norm_two_shift,
        time_qkv,
        time_qv_bias,
        time_out,
        time_out_bias,
        norm_three_gain,
        norm_three_shift,
        mlp_in,
        mlp_in_bias,
        mlp_out,
        mlp_out_bias,
    )
    per_batch = inputs.shape[0] // MICRO
    results = []
    grad_parts = []
    total = None
    for index in range(MICRO):
        full = (
            lax.all_gather(shards[0], ("dp", "seq"), axis=0, tiled=True),
            lax.all_gather(shards[1], ("dp", "seq"), axis=0, tiled=True),
            lax.all_gather(shards[2], ("dp", "seq"), axis=0, tiled=True),
            lax.all_gather(shards[3], ("dp", "seq"), axis=0, tiled=True),
            lax.all_gather(shards[4], ("dp", "seq"), axis=0, tiled=True),
            lax.all_gather(shards[5], ("dp", "seq"), axis=0, tiled=True),
            lax.all_gather(shards[6], ("dp", "seq"), axis=0, tiled=True),
            lax.all_gather(shards[7], ("dp", "seq"), axis=0, tiled=True),
            lax.all_gather(shards[8], ("dp", "seq"), axis=0, tiled=True),
            lax.all_gather(shards[9], ("dp", "seq"), axis=0, tiled=True),
            lax.all_gather(shards[10], ("dp", "seq"), axis=0, tiled=True),
            lax.all_gather(shards[11], ("dp", "seq"), axis=0, tiled=True),
            lax.all_gather(shards[12], ("dp", "seq"), axis=0, tiled=True),
            lax.all_gather(shards[13], ("dp", "seq"), axis=0, tiled=True),
            lax.all_gather(shards[14], ("dp", "seq"), axis=0, tiled=True),
            lax.all_gather(shards[15], ("dp", "seq"), axis=0, tiled=True),
            lax.all_gather(shards[16], ("dp", "seq"), axis=0, tiled=True),
            lax.all_gather(shards[17], ("dp", "seq"), axis=0, tiled=True),
        )
        result, saved = forward(inputs[index * per_batch : (index + 1) * per_batch], full)
        results.append(result)
    for index in range(MICRO):
        full = (
            lax.all_gather(shards[0], ("dp", "seq"), axis=0, tiled=True),
            lax.all_gather(shards[1], ("dp", "seq"), axis=0, tiled=True),
            lax.all_gather(shards[2], ("dp", "seq"), axis=0, tiled=True),
            lax.all_gather(shards[3], ("dp", "seq"), axis=0, tiled=True),
            lax.all_gather(shards[4], ("dp", "seq"), axis=0, tiled=True),
            lax.all_gather(shards[5], ("dp", "seq"), axis=0, tiled=True),
            lax.all_gather(shards[6], ("dp", "seq"), axis=0, tiled=True),
            lax.all_gather(shards[7], ("dp", "seq"), axis=0, tiled=True),
            lax.all_gather(shards[8], ("dp", "seq"), axis=0, tiled=True),
            lax.all_gather(shards[9], ("dp", "seq"), axis=0, tiled=True),
            lax.all_gather(shards[10], ("dp", "seq"), axis=0, tiled=True),
            lax.all_gather(shards[11], ("dp", "seq"), axis=0, tiled=True),
            lax.all_gather(shards[12], ("dp", "seq"), axis=0, tiled=True),
            lax.all_gather(shards[13], ("dp", "seq"), axis=0, tiled=True),
            lax.all_gather(shards[14], ("dp", "seq"), axis=0, tiled=True),
            lax.all_gather(shards[15], ("dp", "seq"), axis=0, tiled=True),
            lax.all_gather(shards[16], ("dp", "seq"), axis=0, tiled=True),
            lax.all_gather(shards[17], ("dp", "seq"), axis=0, tiled=True),
        )
        result, saved = forward(inputs[index * per_batch : (index + 1) * per_batch], full)
        grad_block, terms = backward(
            saved, cotangent[index * per_batch : (index + 1) * per_batch], full
        )
        grad_parts.append(grad_block)
        total = add_terms(total, terms)
    partial_rows = jax.tree.map(
        lambda part: part.astype(jnp.float32),
        lax.psum_scatter(as_sent(total), "dp", scatter_dimension=0, tiled=True),
    )
    owned = jax.tree.map(
        lambda part: part.astype(jnp.float32),
        lax.psum_scatter(as_sent(partial_rows), "seq", scatter_dimension=0, tiled=True),
    )
    return (jnp.concatenate(results, axis=0), jnp.concatenate(grad_parts, axis=0)) + tuple(owned)


def solution(mesh):
    return jax.shard_map(
        on_device,
        mesh=mesh,
        in_specs=(
            P("dp", "seq", None, None),
            P(("dp", "seq")),
            P(("dp", "seq")),
            P(("dp", "seq"), None),
            P(("dp", "seq")),
            P(("dp", "seq"), None),
            P(("dp", "seq")),
            P(("dp", "seq")),
            P(("dp", "seq")),
            P(("dp", "seq"), None),
            P(("dp", "seq")),
            P(("dp", "seq"), None),
            P(("dp", "seq")),
            P(("dp", "seq")),
            P(("dp", "seq")),
            P(("dp", "seq"), None),
            P(("dp", "seq")),
            P(("dp", "seq"), None),
            P(("dp", "seq")),
            P("dp", "seq", None, None),
        ),
        out_specs=(
            P("dp", "seq", None, None),
            P("dp", "seq", None, None),
            P(("dp", "seq")),
            P(("dp", "seq")),
            P(("dp", "seq"), None),
            P(("dp", "seq")),
            P(("dp", "seq"), None),
            P(("dp", "seq")),
            P(("dp", "seq")),
            P(("dp", "seq")),
            P(("dp", "seq"), None),
            P(("dp", "seq")),
            P(("dp", "seq"), None),
            P(("dp", "seq")),
            P(("dp", "seq")),
            P(("dp", "seq")),
            P(("dp", "seq"), None),
            P(("dp", "seq")),
            P(("dp", "seq"), None),
            P(("dp", "seq")),
        ),
        check_vma=False,
    )
```

profile of v0, /device:TPU:0, one launch (start us, length us, event | category | flops | bytes accessed | tf_op | source)
XLA Modules:
  0.0 1215.2 jit_solution(1542048236866879495)
XLA Ops:
  16.7 43.4 %all-reduce.36 = (bf16[768]{0:T(1024)(128)(2,1)S(1)}, bf16[768]{0:T(1024)(128)(2,1)S(1)}, bf16[1536]{0:T(1024)(128)(2,1)S(1)}, bf16[768]{0:T(1024)(128)(2,1)S(1)...) all-reduce(bf16[768]{0:T(1024)(128)(2,1)S(1)} %dynamic-update-slice, ...), channel_id=1, replica_groups=mesh['dp'=8,'seq'=4] {'dp','seq'}, use_global_device_ids=true, to_apply=%add.1 | all-reduce | flops 13056 | bytes 52224
  88.9 8.9 reshape.564
  172.5 42.2 %all-to-all-done.2 = bf16[1,4,256,768]{3,1,0,2:T(4,128)(2,1)} async-done(((bf16[1,4,256,768]{3,1,0,2:T(4,128)(2,1)}), bf16[1,4,256,768]{3,1,0,2:T(4,128)(2,1)}, u32[]{:S(2)}, u32[]{:S(2)}) %all-to-all-start.2) | async-done | bytes 1572896 | tf_op jit(solution)/shard_map/all_to_all | solution.py:152
  231.5 15.0 %reshape.568 = bf16[64,16,3,12,64]{4,3,2,1,0:T(8,128)(2,1)} reshape(bf16[1024,2304]{1,0:T(8,128)(2,1)} %add_convert_fusion.4) | data formatting | bytes 9437184 | tf_op jit(solution)/shard_map/reshape | solution.py:67
  300.9 15.0 %reshape.559 = bf16[64,16,3,12,64]{4,3,2,1,0:T(8,128)(2,1)} reshape(bf16[1024,2304]{1,0:T(8,128)(2,1)} %add_convert_fusion.6) | data formatting | bytes 9437184 | tf_op jit(solution)/shard_map/reshape | solution.py:67
  365.5 36.5 %all-to-all-done.1 = bf16[1,16,64,768]{3,2,0,1:T(8,128)(2,1)} async-done(((bf16[1,16,64,768]{3,2,0,1:T(8,128)(2,1)}), bf16[1,16,64,768]{3,2,0,1:T(8,128)(2,1)}, u32[]{:S(2)}, u32[]{:S(2)}) %all-to-all-start.1) | async-done | bytes 1572896 | tf_op jit(solution)/shard_map/all_to_all | solution.py:159
  426.6 63.1 %multiply_convert_fusion.3 = (bf16[1024,3072]{1,0:T(8,128)(2,1)}, f32[1024,3072]{1,0:T(8,128)}, bf16[1024,3072]{1,0:T(8,128)(2,1)}, f32[1024,3072]{1,0:T(8,128)}, f32[1024,3072]{1,0:T(8,128)}) fusion(f32[3072]{0:T(1024)S(1)} %convert_element_type.617, f32[1024,3072]{1,0:T(8,128)S(1)} %fusion.107, bf16[768,3072]{1,0:T(8,128)(2,1)S(1)} %copy-done.133, ...), kind=kOutput, calls=%fused_computation.31 | convolution fusion | flops 5251006464 | bytes 70805504 | tf_op jit(solution)/shard_map/dot_general | solution.py:165
  489.6 18.9 %convert_reduce_fusion.3 = (f32[3072]{0:T(1024)}, bf16[1024,3072]{1,0:T(8,128)(2,1)}) fusion(f32[1024,3072]{1,0:T(8,128)} %get-tuple-element.103, bf16[1024,768]{1,0:T(8,128)(2,1)} %bitcast.482, bf16[3072,768]{1,0:T(8,128)(2,1)} %all-gather.17.cloned.1.call-done, f32[1024,3072]{1,0:T(8,128)} %get-tuple-element.178, f32[3072]{0:T(1024)S(1)} %convert_element_type.617), kind=kOutput, calls=%fused_computation.9 | convolution fusion | flops 4885312512 | bytes 37773312 | tf_op jit(solution)/shard_map/dot_general | solution.py:34
  508.6 10.9 multiply_reduce_fusion.9
  519.5 18.9 %convert_reduce_fusion.2 = (f32[3072]{0:T(1024)}, bf16[1024,3072]{1,0:T(8,128)(2,1)}) fusion(f32[1024,3072]{1,0:T(8,128)} %get-tuple-element.141, bf16[1024,768]{1,0:T(8,128)(2,1)} %bitcast.451, bf16[3072,768]{1,0:T(8,128)(2,1)} %all-gather.17.cloned.1.call-done, f32[1024,3072]{1,0:T(8,128)} %copy-done.155, f32[3072]{0:T(1024)S(1)} %convert_element_type.617), kind=kOutput, calls=%fused_computation.8 | convolution fusion | flops 4885312512 | bytes 37773312 | tf_op jit(solution)/shard_map/dot_general | solution.py:34
  538.4 14.0 %fusion.108 = (bf16[1024,768]{1,0:T(8,128)(2,1)S(1)}, f32[1024,768]{1,0:T(8,128)}, f32[768]{0:T(1024)}, f32[1024]{0:T(1024)S(1)}, f32[1024]{0:T(1024)S(1)}, /*index=5*/f32[768]{0:T(1024)}, f32[1024,768]{1,0:T(8,128)}) fusion(f32[1024]{0:T(1024)S(1)} %broadcast_multiply_fusion.8, f32[1024,768]{1,0:T(8,128)S(1)} %copy-done.16, ...), kind=kOutput, calls=%fused_computation.316 | convolution fusion | flops 4846776320 | bytes 29926400 | tf_op jit(solution)/shard_map/dot_general | solution.py:34
  565.8 30.8 %all-to-all-done.4 = bf16[1,4,256,768]{3,1,0,2:T(4,128)(2,1)} async-done(((bf16[1,4,256,768]{3,1,0,2:T(4,128)(2,1)}), bf16[1,4,256,768]{3,1,0,2:T(4,128)(2,1)}, u32[]{:S(2)}, u32[]{:S(2)}) %all-to-all-start.4) | async-done | bytes 1572896 | tf_op jit(solution)/shard_map/all_to_all | solution.py:239
  622.3 9.9 multiply_reduce_fusion.5
  651.4 11.0 multiply_reduce_fusion.4
  698.1 16.0 %convert_element_type.666 = bf16[1024,2304]{1,0:T(8,128)(2,1)} reshape(bf16[64,16,3,12,64]{4,3,2,1,0:T(8,128)(2,1)} %copy.250) | data formatting | bytes 9437184 | tf_op jit(solution)/shard_map/convert_element_type | solution.py:107
  742.1 15.6 %convert_element_type.646 = bf16[1024,2304]{1,0:T(8,128)(2,1)} reshape(bf16[64,16,3,12,64]{4,3,2,1,0:T(8,128)(2,1)} %copy.231) | data formatting | bytes 9437184 | tf_op jit(solution)/shard_map/convert_element_type | solution.py:107
  780.9 10.7 fusion.105
  791.6 26.6 %reduce-scatter.25.cloned.1.call-done = bf16[96,768]{1,0:T(8,128)(2,1)} async-done(((bf16[768,768]{1,0:T(8,128)(2,1)}), bf16[96,768]{1,0:T(8,128)(2,1)}) %reduce-scatter.25.cloned.1.call-update) | async-done | bytes 147472 | tf_op jit(solution)/shard_map/reduce_scatter | solution.py:381
  840.6 11.4 add_convert_fusion.3
  861.3 10.4 add_convert_fusion.2
  883.0 10.2 add_convert_fusion.14
  915.3 9.1 multiply_reduce_fusion.1
  960.6 9.8 multiply_reduce_fusion
  1010.2 9.3 add_convert_fusion.10
  1037.4 9.7 fusion.55
  1049.4 22.7 %all-reduce.37 = (bf16[768]{0:T(1024)(128)(2,1)S(1)}, bf16[768]{0:T(1024)(128)(2,1)S(1)}, bf16[1536]{0:T(1024)(128)(2,1)S(1)}, bf16[768]{0:T(1024)(128)(2,1)S(1)...) all-reduce(bf16[768]{0:T(1024)(128)(2,1)S(1)} %add_convert_fusion.2, ...), channel_id=2, replica_groups=mesh['dp'=8,'seq'=4] {'dp'}, use_global_device_ids=true, to_apply=%region_38.0.clone | all-reduce | flops 13056 | bytes 52224
  1073.0 11.8 all-reduce.38
  1104.7 13.6 %reduce-scatter.19.cloned.1.call-done = bf16[24,768]{1,0:T(8,128)(2,1)} async-done(((bf16[96,768]{1,0:T(8,128)(2,1)}), bf16[24,768]{1,0:T(8,128)(2,1)}) %reduce-scatter.19.cloned.1.call-update) | async-done | bytes 36880 | tf_op jit(solution)/shard_map/reduce_scatter | solution.py:385
  1119.8 21.1 %reduce-scatter.31.cloned.1.call-done = bf16[24,3072]{1,0:T(8,128)(2,1)} async-done(((bf16[96,3072]{1,0:T(8,128)(2,1)}), bf16[24,3072]{1,0:T(8,128)(2,1)}) %reduce-scatter.31.cloned.1.call-update) | async-done | bytes 147472 | tf_op jit(solution)/shard_map/reduce_scatter | solution.py:385
  1142.5 20.9 %reduce-scatter.35.cloned.1.call-done = bf16[96,768]{1,0:T(8,128)(2,1)} async-done(((bf16[384,768]{1,0:T(8,128)(2,1)}), bf16[96,768]{1,0:T(8,128)(2,1)}) %reduce-scatter.35.cloned.1.call-update) | async-done | bytes 147472 | tf_op jit(solution)/shard_map/reduce_scatter | solution.py:385
  1165.0 19.9 %reduce-scatter.23.cloned.1.call-done = bf16[24,2304]{1,0:T(8,128)(2,1)} async-done(((bf16[96,2304]{1,0:T(8,128)(2,1)}), bf16[24,2304]{1,0:T(8,128)(2,1)}) %reduce-scatter.23.cloned.1.call-update) | async-done | bytes 110608 | tf_op jit(solution)/shard_map/reduce_scatter | solution.py:385
  1186.5 20.1 %reduce-scatter.15.cloned.1.call-done = bf16[24,2304]{1,0:T(8,128)(2,1)} async-done(((bf16[96,2304]{1,0:T(8,128)(2,1)}), bf16[24,2304]{1,0:T(8,128)(2,1)}) %reduce-scatter.15.cloned.1.call-update) | async-done | bytes 110608 | tf_op jit(solution)/shard_map/reduce_scatter | solution.py:385
  (687 shorter events, 586.7 us)
Async XLA Ops:
  7.2 66.5 %all-gather.7.cloned.1.call-start = ((), (), s32[]{:S(2)}) async-start(), calls=%async_computation.20 | async-start | bytes 3649536 | tf_op jit(solution)/shard_map/all_gather | solution.py:333
  7.9 141.5 %all-gather.9.cloned.1.call-start = ((), (), s32[]{:S(2)}) async-start(), calls=%async_computation.21 | async-start | bytes 1216512 | tf_op jit(solution)/shard_map/all_gather | solution.py:335
  8.7 214.3 %all-gather.11.cloned.1.call-start = ((), (), s32[]{:S(2)}) async-start(), calls=%async_computation.22 | async-start | bytes 3649536 | tf_op jit(solution)/shard_map/all_gather | solution.py:339
  62.6 96.1 %copy-start.92 = (f32[768]{0:T(1024)}, f32[768]{0:T(1024)S(1)}, u32[]{:S(2)}) copy-start(f32[768]{0:T(1024)S(1)} %convert_element_type.600) | copy-start | bytes 9220
  153.4 252.3 %copy-start.6 = (f32[1024,768]{1,0:T(8,128)}, f32[1024,768]{1,0:T(8,128)S(1)}, u32[]{:S(2)}) copy-start(f32[1024,768]{1,0:T(8,128)S(1)} %get-tuple-element.173) | copy-start | bytes 9437188
  163.2 51.6 %all-to-all-start.2 = ((bf16[1,4,256,768]{3,1,0,2:T(4,128)(2,1)}), bf16[1,4,256,768]{3,1,0,2:T(4,128)(2,1)}, u32[]{:S(2)}, u32[]{:S(2)}) async-start(bf16[1,4,256,768]{3,1,0,2:T(4,128)(2,1)} %copy.212), calls=%async_computation.2 | async-start | bytes 3145728 | tf_op jit(solution)/shard_map/all_to_all | solution.py:152
  167.5 114.6 %all-gather.13.cloned.1.call-start = ((), (), s32[]{:S(2)}) async-start(), calls=%async_computation.23 | async-start | bytes 1216512 | tf_op jit(solution)/shard_map/all_gather | solution.py:341
  168.1 245.3 %all-gather.15.cloned.1.call-start = ((), (), s32[]{:S(2)}) async-start(), calls=%async_computation.24 | async-start | bytes 4866048 | tf_op jit(solution)/shard_map/all_gather | solution.py:345
  214.7 72.1 %all-to-all-start = ((bf16[1,4,256,768]{3,1,0,2:T(4,128)(2,1)}), bf16[1,4,256,768]{3,1,0,2:T(4,128)(2,1)}, u32[]{:S(2)}, u32[]{:S(2)}) async-start(bf16[1,4,256,768]{3,1,0,2:T(4,128)(2,1)} %copy.194), calls=%async_computation | async-start | bytes 3145728 | tf_op jit(solution)/shard_map/all_to_all | solution.py:152
  286.9 65.5 %all-to-all-start.3 = ((bf16[1,16,64,768]{3,2,0,1:T(8,128)(2,1)}), bf16[1,16,64,768]{3,2,0,1:T(8,128)(2,1)}, u32[]{:S(2)}, u32[]{:S(2)}) async-start(bf16[1,16,64,768]{3,2,0,1:T(8,128)(2,1)} %bitcast.437), calls=%async_computation.3 | async-start | bytes 3145728 | tf_op jit(solution)/shard_map/all_to_all | solution.py:159
  352.4 49.7 %all-to-all-start.1 = ((bf16[1,16,64,768]{3,2,0,1:T(8,128)(2,1)}), bf16[1,16,64,768]{3,2,0,1:T(8,128)(2,1)}, u32[]{:S(2)}, u32[]{:S(2)}) async-start(bf16[1,16,64,768]{3,2,0,1:T(8,128)(2,1)} %bitcast.438), calls=%async_computation.1 | async-start | bytes 3145728 | tf_op jit(solution)/shard_map/all_to_all | solution.py:159
  357.4 132.3 %all-gather.17.cloned.1.call-start = ((), (), s32[]{:S(2)}) async-start(), calls=%async_computation.25 | async-start | bytes 4866048 | tf_op jit(solution)/shard_map/all_gather | solution.py:347
  358.0 63.7 %copy-start.82 = (f32[768]{0:T(1024)}, f32[768]{0:T(1024)S(1)}, u32[]{:S(2)}) copy-start(f32[768]{0:T(1024)S(1)} %convert_element_type.615) | copy-start | bytes 9220
  519.5 18.9 %copy-start.12 = (f32[1024,768]{1,0:T(8,128)S(1)}, f32[1024,768]{1,0:T(8,128)}, u32[]{:S(2)}) copy-start(f32[1024,768]{1,0:T(8,128)} %copy-done.11) | copy-start | bytes 9437188
  519.5 18.9 %copy-start.16 = (f32[1024,768]{1,0:T(8,128)S(1)}, f32[1024,768]{1,0:T(8,128)}, u32[]{:S(2)}) copy-start(f32[1024,768]{1,0:T(8,128)} %copy-done.14) | copy-start | bytes 9437188
  519.5 18.9 %copy-start.85 = (f32[1024]{0:T(1024)S(1)}, f32[1024]{0:T(1024)}, u32[]{:S(2)}) copy-start(f32[1024]{0:T(1024)} %copy-done.84) | copy-start | bytes 12292
  554.9 41.7 %all-to-all-start.4 = ((bf16[1,4,256,768]{3,1,0,2:T(4,128)(2,1)}), bf16[1,4,256,768]{3,1,0,2:T(4,128)(2,1)}, u32[]{:S(2)}, u32[]{:S(2)}) async-start(bf16[1,4,256,768]{3,1,0,2:T(4,128)(2,1)} %copy.224), calls=%async_computation.4 | async-start | bytes 3145728 | tf_op jit(solution)/shard_map/all_to_all | solution.py:239
  596.5 41.1 %all-to-all-start.6 = ((bf16[1,4,256,768]{3,1,0,2:T(4,128)(2,1)}), bf16[1,4,256,768]{3,1,0,2:T(4,128)(2,1)}, u32[]{:S(2)}, u32[]{:S(2)}) async-start(bf16[1,4,256,768]{3,1,0,2:T(4,128)(2,1)} %copy.243), calls=%async_computation.6 | async-start | bytes 3145728 | tf_op jit(solution)/shard_map/all_to_all | solution.py:239
  723.0 47.5 %all-to-all-start.7 = ((bf16[1,16,64,768]{3,2,0,1:T(8,128)(2,1)}), bf16[1,16,64,768]{3,2,0,1:T(8,128)(2,1)}, u32[]{:S(2)}, u32[]{:S(2)}) async-start(bf16[1,16,64,768]{3,2,0,1:T(8,128)(2,1)} %bitcast.439), calls=%async_computation.7 | async-start | bytes 3145728 | tf_op jit(solution)/shard_map/all_to_all | solution.py:246
  770.4 49.7 %all-to-all-start.5 = ((bf16[1,16,64,768]{3,2,0,1:T(8,128)(2,1)}), bf16[1,16,64,768]{3,2,0,1:T(8,128)(2,1)}, u32[]{:S(2)}, u32[]{:S(2)}) async-start(bf16[1,16,64,768]{3,2,0,1:T(8,128)(2,1)} %bitcast.414), calls=%async_computation.5 | async-start | bytes 3145728 | tf_op jit(solution)/shard_map/all_to_all | solution.py:246
  775.5 42.8 %reduce-scatter.25.cloned.1.call-start = ((), (), s32[]{:S(2)}) async-start(), calls=%async_computation.32 | async-start | bytes 1327104 | tf_op jit(solution)/shard_map/reduce_scatter | solution.py:381
  780.8 244.6 %reduce-scatter.27.cloned.1.call-start = ((), (), s32[]{:S(2)}) async-start(), calls=%async_computation.33 | async-start | bytes 184320 | tf_op jit(solution)/shard_map/reduce_scatter | solution.py:385
  818.3 228.8 %reduce-scatter.17.cloned.1.call-start = ((), (), s32[]{:S(2)}) async-start(), calls=%async_computation.28 | async-start | bytes 1327104 | tf_op jit(solution)/shard_map/reduce_scatter | solution.py:381
  840.6 208.3 %reduce-scatter.29.cloned.1.call-start = ((), (), s32[]{:S(2)}) async-start(), calls=%async_computation.34 | async-start | bytes 5308416 | tf_op jit(solution)/shard_map/reduce_scatter | solution.py:381
  852.1 233.3 %reduce-scatter.33.cloned.1.call-start = ((), (), s32[]{:S(2)}) async-start(), calls=%async_computation.36 | async-start | bytes 5308416 | tf_op jit(solution)/shard_map/reduce_scatter | solution.py:381
  871.8 220.1 %reduce-scatter.21.cloned.1.call-start = ((), (), s32[]{:S(2)}) async-start(), calls=%async_computation.30 | async-start | bytes 3981312 | tf_op jit(solution)/shard_map/reduce_scatter | solution.py:381
  902.9 194.1 %reduce-scatter.13.cloned.1.call-start = ((), (), s32[]{:S(2)}) async-start(), calls=%async_computation.26 | async-start | bytes 3981312 | tf_op jit(solution)/shard_map/reduce_scatter | solution.py:381
  1010.2 108.2 %reduce-scatter.19.cloned.1.call-start = ((), (), s32[]{:S(2)}) async-start(), calls=%async_computation.29 | async-start | bytes 184320 | tf_op jit(solution)/shard_map/reduce_scatter | solution.py:385
  1047.1 93.7 %reduce-scatter.31.cloned.1.call-start = ((), (), s32[]{:S(2)}) async-start(), calls=%async_computation.35 | async-start | bytes 737280 | tf_op jit(solution)/shard_map/reduce_scatter | solution.py:385
  1048.9 114.4 %reduce-scatter.35.cloned.1.call-start = ((), (), s32[]{:S(2)}) async-start(), calls=%async_computation.37 | async-start | bytes 737280 | tf_op jit(solution)/shard_map/reduce_scatter | solution.py:385
  1085.4 99.5 %reduce-scatter.23.cloned.1.call-start = ((), (), s32[]{:S(2)}) async-start(), calls=%async_computation.31 | async-start | bytes 552960 | tf_op jit(solution)/shard_map/reduce_scatter | solution.py:385
  1091.9 114.6 %reduce-scatter.15.cloned.1.call-start = ((), (), s32[]{:S(2)}) async-start(), calls=%async_computation.27 | async-start | bytes 552960 | tf_op jit(solution)/shard_map/reduce_scatter | solution.py:385
  (168 other events, 844.4 us)
Sparse Core Ops, SparseCore 0:
  10.8 62.8 all-gather.6
  76.5 53.0 all-gather.8
  132.4 64.6 all-gather.10
  199.7 82.3 all-gather.12
  284.8 92.8 all-gather.14
  380.3 62.9 all-gather.16
  780.9 37.2 reduce-scatter.24
  820.6 19.2 reduce-scatter.26
  843.1 34.9 reduce-scatter.16
  881.8 53.8 reduce-scatter.28
  939.2 53.8 reduce-scatter.32
  996.8 48.0 reduce-scatter.20
  1048.8 48.1 reduce-scatter.12
  1099.2 19.1 reduce-scatter.18
  1120.5 20.2 reduce-scatter.30
  1143.0 20.3 reduce-scatter.34
  1165.5 19.3 reduce-scatter.22
  1187.1 19.3 reduce-scatter.14
where the time goes:
time: 1220 us
  matrix products  423 us (35%)
  local copies, waits for them, and re-layouts  280 us (23%)
  waiting for transfers between devices  258 us (21%)
  other arithmetic  118 us (10%)
  blocking collectives  77.9 us (6%)
  starting transfers between devices  37.6 us (3%)
  between operations  21 us (2%)
    dot_general x12, matrix products, back_dot(): lax.dot_general(grad, weight, (((1,), (1,)), ((), ())), preferred_element...  107 us
    reduce_scatter x6, waiting for transfers between devices, on_device(): lax.psum_scatter(as_sent(partial_rows), 'seq', scatter_dimension=0, tiled...  95.5 us
    unnamed x3, blocking collectives  77.9 us
    dot_general x12, matrix products, outer_sum(): lax.dot_general(left, right, (((0,), (0,)), ((), ())), preferred_element_...  75.7 us
    dot_general x2, matrix products, forward(): jnp.dot(mlp_rows, mlp_in, preferred_element_type=jnp.float32)  71.4 us
    unnamed x394, local copies, waits for them, and re-layouts  53.9 us
    convert_element_type x6, local copies, waits for them, and re-layouts, attend_back(): jnp.stack([grad_query, grad_keys, grad_values], axis=2).astype(jnp.bfloat16)  53.7 us
    reshape x4, local copies, waits for them, and re-layouts, attend(): project = project.reshape(seq_count, length, 3, HEADS, HD)  47.7 us
  transfers between devices with their start and end apart: 26, of which 13 were waited for; matrix products, arithmetic and copies ran while one was open for 52% of the time, Pallas kernels for 0%

commit v1 on v0

v1 whole, which is shorter than its diff:
```python
import functools
import jax
import jax.numpy as jnp
from jax import lax
from jax.experimental import pallas as pl
from jax.experimental.pallas import tpu as pltpu
from jax.sharding import PartitionSpec as P

HEADS = 12
HD = 64
EPS = 1e-06
SCALE = 0.125
F32 = jnp.float32
BF16 = jnp.bfloat16
RSQRT2 = 0.7071067811865476
RSQRT2PI = 0.3989422804014327


def dot(a, b):
    return jnp.dot(a, b, preferred_element_type=F32)


def dot_nt(a, b):
    return lax.dot_general(a, b, (((1,), (1,)), ((), ())), preferred_element_type=F32)


def fold(rows):
    return jnp.sum(rows.reshape(rows.shape[0] // 8, 8, rows.shape[1]), axis=0)


def norm(rows):
    center = rows - jnp.mean(rows, axis=-1, keepdims=True)
    rstd = lax.rsqrt(jnp.mean(center * center, axis=-1, keepdims=True) + EPS)
    return center * rstd, rstd


def norm_back(du, hat, rstd, gain):
    e = du * gain
    return rstd * (
        e - jnp.mean(e, axis=-1, keepdims=True) - hat * jnp.mean(e * hat, axis=-1, keepdims=True)
    )


def split_heads(pair):
    low = lax.broadcasted_iota(jnp.int32, (1, 2 * HD), 1) < HD
    zero = jnp.zeros_like(pair)
    return jnp.concatenate([jnp.where(low, pair, zero), jnp.where(low, zero, pair)], axis=0)


def join_heads(both):
    n = both.shape[0] // 2
    low = lax.broadcasted_iota(jnp.int32, (1, 2 * HD), 1) < HD
    return jnp.where(low, both[:n], both[n:])


def by_head(left, right):
    n = right.shape[0] // 2
    top = dot(left[:HD], right[:n])
    bottom = dot(left[HD:], right[n:])
    return jnp.concatenate([top, bottom], axis=0)


def attend(qkv_ref, pt_ref, o_ref, period):
    width = HEADS * HD
    n = qkv_ref.shape[0]
    for pair in range(HEADS // 2):
        at = pair * 2 * HD
        q = qkv_ref[:, at : at + 2 * HD] * jnp.asarray(SCALE, BF16)
        k = qkv_ref[:, width + at : width + at + 2 * HD]
        v = qkv_ref[:, 2 * width + at : 2 * width + at + 2 * HD]
        s = dot_nt(split_heads(k), q)
        if period:
            keys = lax.broadcasted_iota(jnp.int32, s.shape, 0) % period
            queries = lax.broadcasted_iota(jnp.int32, s.shape, 1) % period
            s = jnp.where(keys == queries, s, -1e30)
        probs = []
        for half in (s[:n], s[n:]):
            e = jnp.exp(half - jnp.max(half, axis=0, keepdims=True))
            probs.append((e * (1.0 / jnp.sum(e, axis=0, keepdims=True))).astype(BF16))
        p = jnp.concatenate(probs, axis=0)
        pt_ref[pair] = p
        o_ref[:, at : at + 2 * HD] = by_head(v.T, p).astype(BF16).T


def attend_back(qkv_ref, pt_ref, do, dp_ref):
    width = HEADS * HD
    n = qkv_ref.shape[0]
    for pair in range(HEADS // 2):
        at = pair * 2 * HD
        q = qkv_ref[:, at : at + 2 * HD] * jnp.asarray(SCALE, BF16)
        k = qkv_ref[:, width + at : width + at + 2 * HD]
        v = qkv_ref[:, 2 * width + at : 2 * width + at + 2 * HD]
        g = do[:, at : at + 2 * HD]
        p = pt_ref[pair]
        dp = dot_nt(split_heads(v), g)
        wide = p.astype(F32)
        ds = []
        for sl in (slice(0, n), slice(n, 2 * n)):
            t = wide[sl] * dp[sl]
            ds.append((t - wide[sl] * jnp.sum(t, axis=0, keepdims=True)).astype(BF16))
        ds = jnp.concatenate(ds, axis=0)
        dp_ref[:, 2 * width + at : 2 * width + at + 2 * HD] = join_heads(dot(p, g)).astype(BF16)
        dp_ref[:, width + at : width + at + 2 * HD] = join_heads(dot(ds, q)).astype(BF16)
        dp_ref[:, at : at + 2 * HD] = (by_head(k.T, ds) * SCALE).astype(BF16).T


GAIN1, SHIFT1, BO1, GAIN2, SHIFT2, BO2, GAIN3, SHIFT3, BOUT, BQ1, BV1, BQ2, BV2, BIN = range(14)
NARROW = (0, 1, 3, 4, 5, 7, 8, 9, 11)
WIDE = (2, 6)
LONG = 10
VEC_ROWS = 32
SUM_ROWS = 24
VMEM_LIMIT = 60 * 2**20


def row(vec_ref, i):
    return vec_ref[i : i + 1]


def project(a, wqkv_ref, bq, bv, qkv_ref):
    width = a.shape[1]
    for i, bias in enumerate((bq, None, bv)):
        sl = slice(i * width, (i + 1) * width)
        part = dot(a, wqkv_ref[:, sl])
        qkv_ref[:, sl] = (part if bias is None else part + bias).astype(BF16)


def space_rows(x, vec_ref, wqkv_ref, wo_ref, a_ref, qkv_ref, pt_ref, o_ref):
    hat, _ = norm(x)
    a = (hat * row(vec_ref, GAIN1) + row(vec_ref, SHIFT1)).astype(BF16)
    a_ref[...] = a
    project(a, wqkv_ref, row(vec_ref, BQ1), row(vec_ref, BV1), qkv_ref)
    attend(qkv_ref, pt_ref, o_ref, 0)
    return (x + dot(o_ref[...], wo_ref[...]) + row(vec_ref, BO1)).astype(BF16)


def place_rows(
    x1, g16, period, vec_ref, wqkv_ref, wo_ref, win_ref, wout_ref, a2_ref, dp_ref, o_ref, gt_ref, a3_ref, z_ref, dh_ref,
    sum_ref, qkv_ref, pt_ref,
):
    rows, width = x1.shape
    hat2, rstd2 = norm(x1)
    a2 = (hat2 * row(vec_ref, GAIN2) + row(vec_ref, SHIFT2)).astype(BF16)
    a2_ref[...] = a2
    project(a2, wqkv_ref, row(vec_ref, BQ2), row(vec_ref, BV2), qkv_ref)
    attend(qkv_ref, pt_ref, o_ref, period)
    t = (dot(o_ref[...], wo_ref[...]) + row(vec_ref, BO2)).astype(BF16).astype(F32)
    x2 = x1 + t
    hat3, rstd3 = norm(x2)
    a3 = (hat3 * row(vec_ref, GAIN3) + row(vec_ref, SHIFT3)).astype(BF16)
    a3_ref[...] = a3
    g = g16.astype(F32)
    sum_ref[BOUT] += fold(g)
    y = x2 + row(vec_ref, BOUT)
    da3 = jnp.zeros((rows, width), F32)
    for i in range(win_ref.shape[1] // width):
        sl = slice(i * width, (i + 1) * width)
        h = dot(a3, win_ref[:, sl]) + row(vec_ref, BIN + i)
        cdf = 0.5 + 0.5 * lax.erf(h * RSQRT2)
        z = (h * cdf).astype(BF16)
        z_ref[:, sl] = z
        y = y + dot(z, wout_ref[sl, :])
        dz = dot_nt(g16, wout_ref[sl, :])
        dh = (dz * (cdf + h * (RSQRT2PI * jnp.exp(-0.5 * h * h)))).astype(BF16)
        dh_ref[:, sl] = dh
        sum_ref[BIN + i] += fold(dh.astype(F32))
        da3 = da3 + dot_nt(dh, win_ref[:, sl])
    sum_ref[GAIN3] += fold(da3 * hat3)
    sum_ref[SHIFT3] += fold(da3)
    dx2 = g + norm_back(da3, hat3, rstd3, row(vec_ref, GAIN3))
    gt = dx2.astype(BF16)
    gt_ref[...] = gt
    sum_ref[BO2] += fold(gt.astype(F32))
    do = dot_nt(gt, wo_ref[...]).astype(BF16)
    attend_back(qkv_ref, pt_ref, do, dp_ref)
    sum_ref[BQ2] += fold(dp_ref[:, :width].astype(F32))
    sum_ref[BV2] += fold(dp_ref[:, 2 * width :].astype(F32))
    da2 = dot_nt(dp_ref[...], wqkv_ref[...]).astype(BF16).astype(F32)
    sum_ref[GAIN2] += fold(da2 * hat2)
    sum_ref[SHIFT2] += fold(da2)
    dx1 = dx2 + norm_back(da2, hat2, rstd2, row(vec_ref, GAIN2))
    return y.astype(BF16), dx1.astype(BF16)


def space_back_rows(x, g, qkv_ref, pt_ref, vec_ref, wqkv_ref, wo_ref, dp_ref, sum_ref):
    width = x.shape[1]
    sum_ref[BO1] += fold(g.astype(F32))
    do = dot_nt(g, wo_ref[...]).astype(BF16)
    attend_back(qkv_ref, pt_ref, do, dp_ref)
    sum_ref[BQ1] += fold(dp_ref[:, :width].astype(F32))
    sum_ref[BV1] += fold(dp_ref[:, 2 * width :].astype(F32))
    da = dot_nt(dp_ref[...], wqkv_ref[...])
    hat, rstd = norm(x)
    sum_ref[GAIN1] += fold(da * hat)
    sum_ref[SHIFT1] += fold(da)
    return (g.astype(F32) + norm_back(da, hat, rstd, row(vec_ref, GAIN1))).astype(BF16)


def params(collective=None):
    extra = {} if collective is None else {"collective_id": collective, "has_side_effects": True}
    return pltpu.CompilerParams(vmem_limit_bytes=VMEM_LIMIT, dimension_semantics=("arbitrary",), **extra)


def whole(shape):
    return pl.BlockSpec(shape, lambda b: (0,) * len(shape), pipeline_mode=pl.Buffered(1))


def rows_spec(rows, cols):
    return pl.BlockSpec((rows, cols), lambda b: (b, 0))


def sds(*shape, dtype=BF16):
    return jax.ShapeDtypeStruct(shape, dtype)


ANYWHERE = pl.BlockSpec(memory_space=pl.ANY)


def space_kernel(x_ref, vec_ref, wqkv_ref, wo_ref, x1_ref, a_ref, qkv_ref, pt_ref, o_ref):
    x1_ref[0] = space_rows(x_ref[0].astype(F32), vec_ref, wqkv_ref, wo_ref, a_ref, qkv_ref, pt_ref.at[0], o_ref)


def place_kernel(x1_ref, g_ref, vec_ref, wqkv_ref, wo_ref, win_ref, wout_ref, out_ref, dx1_ref, *rest):
    _, frames, places, width = x1_ref.shape
    rows = frames * places
    sum_ref = rest[7]

    @pl.when(pl.program_id(0) == 0)
    def _():
        sum_ref[...] = jnp.zeros_like(sum_ref)

    x1 = x1_ref[0].reshape(rows, width).astype(F32)
    g16 = g_ref[0].reshape(rows, width)
    out, dx1 = place_rows(x1, g16, places, vec_ref, wqkv_ref, wo_ref, win_ref, wout_ref, *rest)
    out_ref[0] = out.reshape(frames, places, width)
    dx1_ref[0] = dx1.reshape(frames, places, width)


def space_back_kernel(x_ref, g_ref, qkv_ref, pt_ref, vec_ref, wqkv_ref, wo_ref, dx_ref, dp_ref, sum_ref):
    @pl.when(pl.program_id(0) == 0)
    def _():
        sum_ref[...] = jnp.zeros_like(sum_ref)

    dx_ref[0] = space_back_rows(
        x_ref[0].astype(F32), g_ref[0], qkv_ref, pt_ref.at[0], vec_ref, wqkv_ref, wo_ref, dp_ref, sum_ref
    )


def probs_spec(rows):
    return pl.BlockSpec((1, HEADS // 2, 2 * rows, rows), lambda b: (b, 0, 0, 0))


def space_fwd(x, vec, wqkv, wo):
    blocks, rows, width = x.shape
    tok = blocks * rows
    seq = pl.BlockSpec((1, rows, width), lambda b: (b, 0, 0))
    return pl.pallas_call(
        space_kernel,
        grid=(blocks,),
        in_specs=[seq, whole(vec.shape), whole(wqkv.shape), whole(wo.shape)],
        out_specs=[seq, rows_spec(rows, width), rows_spec(rows, 3 * width), probs_spec(rows), rows_spec(rows, width)],
        out_shape=[
            sds(*x.shape), sds(tok, width), sds(tok, 3 * width), sds(blocks, HEADS // 2, 2 * rows, rows), sds(tok, width)
        ],
        compiler_params=params(),
        name="space_fwd",
    )(x, vec, wqkv, wo)


def place_all(x1, g, vec, wqkv, wo, win, wout):
    clips, frames, places, width = x1.shape
    rows = 256
    part = rows // frames
    per = places // part
    blocks = clips * per
    tok = blocks * rows
    ff = win.shape[1]
    spec = pl.BlockSpec((1, frames, part, width), lambda b: (b // per, 0, b % per, 0))
    n = rows_spec(rows, width)
    return pl.pallas_call(
        place_kernel,
        grid=(blocks,),
        in_specs=[spec, spec] + [whole(w.shape) for w in (vec, wqkv, wo, win, wout)],
        out_specs=[
            spec, spec, n, rows_spec(rows, 3 * width), n, n, n, rows_spec(rows, ff), rows_spec(rows, ff),
            pl.BlockSpec((SUM_ROWS, 8, width), lambda b: (0, 0, 0)),
        ],
        out_shape=[
            sds(*x1.shape), sds(*x1.shape), sds(tok, width), sds(tok, 3 * width), sds(tok, width), sds(tok, width),
            sds(tok, width), sds(tok, ff), sds(tok, ff), sds(SUM_ROWS, 8, width, dtype=F32),
        ],
        scratch_shapes=[pltpu.VMEM((rows, 3 * width), BF16), pltpu.VMEM((HEADS // 2, 2 * rows, rows), BF16)],
        compiler_params=params(),
        name="place_all",
    )(x1, g, vec, wqkv, wo, win, wout)


def space_bwd(x, g, qkv, pt, vec, wqkv, wo):
    blocks, rows, width = x.shape
    tok = blocks * rows
    seq = pl.BlockSpec((1, rows, width), lambda b: (b, 0, 0))
    return pl.pallas_call(
        space_back_kernel,
        grid=(blocks,),
        in_specs=[
            seq, seq, rows_spec(rows, 3 * width), probs_spec(rows), whole(vec.shape), whole(wqkv.shape), whole(wo.shape)
        ],
        out_specs=[seq, rows_spec(rows, 3 * width), pl.BlockSpec((SUM_ROWS, 8, width), lambda b: (0, 0, 0))],
        out_shape=[sds(*x.shape), sds(tok, 3 * width), sds(SUM_ROWS, 8, width, dtype=F32)],
        compiler_params=params(),
        name="space_bwd",
    )(x, g, qkv, pt, vec, wqkv, wo)


def outer_sum(left, right):
    return lax.dot_general(left, right, (((0,), (0,)), ((), ())), preferred_element_type=F32)


def plain_layer(inputs, cotangent, shards, vec):
    clips, frames, places, width = inputs.shape

    def out_there(rows):
        return lax.all_to_all(rows, "seq", split_axis=2, concat_axis=1, tiled=True)

    def back_home(rows):
        return lax.all_to_all(rows, "seq", split_axis=1, concat_axis=2, tiled=True)

    wqkv, wo, tqkv, to, win, wout = [lax.all_gather(s, ("dp", "seq"), axis=0, tiled=True) for s in shards]
    vec = lax.psum(vec, ("dp", "seq"))
    x = inputs.reshape(clips * frames, places, width)
    cot = out_there(cotangent)
    x1, a1, qkv, pt, o = space_fwd(x, vec, wqkv, wo)
    x1 = out_there(x1.reshape(inputs.shape))
    out, dx1, a2, dp, ot, gt, a3, z, dh, sums = place_all(x1, cot, vec, tqkv, to, win, wout)
    output = back_home(out)
    g1 = back_home(dx1).reshape(x.shape)
    dx, dps, space_sums = space_bwd(x, g1, qkv, pt, vec, wqkv, wo)
    part = 256 // cot.shape[1]
    g = cot.reshape(clips, cot.shape[1], -1, part, width).transpose(0, 2, 1, 3, 4).reshape(-1, width)
    pairs = ((a1, dps), (o, g1.reshape(-1, width)), (a2, dp), (ot, gt), (a3, dh), (z, g))
    grads = []
    for left, right in pairs:
        part = lax.psum_scatter(outer_sum(left, right).astype(BF16), "dp", scatter_dimension=0, tiled=True)
        grads.append(lax.psum_scatter(part, "seq", scatter_dimension=0, tiled=True).astype(F32))
    return output, dx.reshape(inputs.shape), grads, lax.psum((sums + space_sums).sum(1), ("dp", "seq"))


MESH = pl.DeviceIdType.MESH


def position():
    d, z = lax.axis_index("dp"), lax.axis_index("seq")
    return d // 4, lax.rem(d // 2, 2), lax.rem(d, 2), z


def partners():
    y, x, c, z = position()
    return {
        "x": (4 * y + 2 * (1 - x) + c, z),
        "y": (4 * (1 - y) + 2 * x + c, z),
        "core": (4 * y + 2 * x + 1 - c, z),
        "z1": (4 * y + 2 * x + c, lax.rem(z + 1, 4)),
        "z2": (4 * y + 2 * x + c, lax.rem(z + 2, 4)),
        "z3": (4 * y + 2 * x + c, lax.rem(z + 3, 4)),
    }


def enter(peers):
    barrier = pltpu.get_barrier_semaphore()
    for peer in peers.values():
        pl.semaphore_signal(barrier, inc=1, device_id=peer, device_id_type=MESH)
    pl.semaphore_wait(barrier, len(peers))


class Sum:
    def __init__(self, peers, held, got, send, recv):
        self.peers, self.held, self.got, self.send, self.recv = peers, held, got, send, recv

    def copy(self, i, kind, level):
        return pltpu.make_async_remote_copy(
            src_ref=self.held.at[level], dst_ref=self.got.at[i], send_sem=self.send.at[i], recv_sem=self.recv.at[i],
            device_id=self.peers[kind], device_id_type=MESH,
        )

    STAGES = ((("z1", 0), ("z2", 1), ("z3", 2)), (("x", 3),), (("y", 4),), (("core", 5),))

    def start(self, level):
        for kind, i in self.STAGES[level]:
            self.copy(i, kind, level).start()

    def finish(self, level):
        total = self.held[level].astype(F32)
        for kind, i in self.STAGES[level]:
            self.copy(i, kind, level).wait_recv()
            total = total + self.got[i].astype(F32)
        self.held[level + 1] = total.astype(self.held.dtype)

    def drain(self):
        for level, stage in enumerate(self.STAGES):
            for kind, i in stage:
                self.copy(i, kind, level).wait_send()


class Gather:
    def __init__(self, peers, shard, zbuf, group, full, local, send, recv):
        self.peers, self.shard, self.zbuf, self.group, self.full = peers, shard, zbuf, group, full
        self.local, self.send, self.recv = local, send, recv
        self.rows, self.cols = group.shape

    def place(self, which, half):
        y, x, c, _ = position()
        y, x = {"own": (y, x), "x": (y, 1 - x), "y": (1 - y, x), "xy": (1 - y, 1 - x)}[which]
        rows = pl.ds(pl.multiple_of((4 * y + 2 * x + c) * self.rows, self.rows), self.rows)
        n = self.cols // 2
        return (rows, slice(None)) if half is None else (rows, pl.ds(half * n, n))

    PLAN = {
        3: ("own", 0, "x"), 4: ("own", 1, "y"), 5: ("own", 0, "y"), 6: ("x", 0, "y"), 7: ("own", 1, "x"), 8: ("y", 1, "x"),
        9: ("own", None, "core"), 10: ("x", 0, "core"), 11: ("y", 1, "core"), 12: ("y", 0, "core"), 13: ("xy", 0, "core"),
        14: ("x", 1, "core"), 15: ("xy", 1, "core"),
    }

    def copy(self, i):
        if i < 3:
            z = lax.axis_index("seq")
            src, dst, kind = self.shard, self.zbuf.at[z], ("z1", "z2", "z3")[i]
        else:
            which, half, kind = self.PLAN[i]
            at = self.place(which, half)
            src = dst = self.full.at[at]
            if which == "own":
                src = self.group if half is None else self.group.at[:, pl.ds(half * (self.cols // 2), self.cols // 2)]
        return pltpu.make_async_remote_copy(
            src_ref=src, dst_ref=dst, send_sem=self.send.at[i], recv_sem=self.recv.at[i], device_id=self.peers[kind],
            device_id_type=MESH,
        )

    def own_in(self):
        return pltpu.make_async_copy(self.shard, self.zbuf.at[lax.axis_index("seq")], self.local.at[0])

    def own_out(self):
        return pltpu.make_async_copy(self.group, self.full.at[self.place("own", None)], self.local.at[1])

    def start(self, items):
        for i in items:
            self.copy(i).start()

    def arrive(self, items):
        for i in items:
            self.copy(i).wait_recv()

    def step0(self):
        self.own_in().start()
        self.start((0, 1, 2))

    def step1(self):
        self.own_in().wait()
        self.arrive((0, 1, 2))
        self.group[...] = jnp.concatenate([self.zbuf[i].astype(F32) for i in range(4)], axis=0).astype(BF16)
        self.own_out().start()
        self.start((3, 4, 5, 7, 9))

    def step2(self):
        self.arrive((3, 4))
        self.start((6, 8, 10, 11))

    def step3(self):
        self.arrive((5, 7, 6, 8))
        self.start((12, 14, 13, 15))

    def step4(self):
        self.arrive((9, 10, 11, 12, 14, 13, 15))
        self.own_out().wait()

    def drain(self):
        for i in range(16):
            self.copy(i).wait_send()


class Swap:
    def __init__(self, peers, pick, land, local, send, recv):
        self.peers, self.pick, self.land, self.local, self.send, self.recv = peers, pick, land, local, send, recv

    def copies(self):
        z = lax.axis_index("seq")
        for j in range(3):
            yield pltpu.make_async_remote_copy(
                src_ref=self.pick(lax.rem(z + j + 1, 4)), dst_ref=self.land, send_sem=self.send.at[j], recv_sem=self.recv.at[j],
                device_id=self.peers[f"z{j + 1}"], device_id_type=MESH,
            )

    def own(self):
        return pltpu.make_async_copy(self.pick(lax.axis_index("seq")), self.land, self.local)

    def start(self):
        for copy in self.copies():
            copy.start()
        self.own().start()

    def arrive(self):
        for copy in self.copies():
            copy.wait_recv()
        self.own().wait()

    def drain(self):
        for copy in self.copies():
            copy.wait_send()


def rows_at(start, size):
    return pl.ds(pl.multiple_of(start, size), size)


BEFORE = {
    0: ("1 0", "1 1", "2 0", "2 1", "1 2", "3 0", "3 1", "1 3", "4 0", "4 1"),
    1: ("2 2", "2 3", "1 4"), 3: ("3 2", "3 3", "1 5"), 5: ("2 4", "4 2", "4 3"), 7: ("2 5", "3 4"),
}
AFTER = ("3 5", "4 4", "4 5")


def first_kernel(x_ref, vec_ref, *refs):
    shards = refs[:6]
    a_ref, qkv_ref, pt_ref, o_ref, land_ref = refs[6:11]
    fulls, vec_out = refs[11:17], refs[17]
    wqkv_ref, wo_ref, x1_ref = refs[18:21]
    zbufs, groups = refs[21:27], refs[27:33]
    held, got, local, send, recv, vsend, vrecv, keep, xlocal, xsend, xrecv = refs[33:]
    step = pl.program_id(0)
    blocks, rows, width = x1_ref.shape
    per = land_ref.shape[1] // 4
    part = rows // 4
    z = lax.axis_index("seq")
    peers = partners()
    vec = Sum(peers, held, got, vsend, vrecv)
    homes = (wqkv_ref, wo_ref) + tuple(fulls[2:])
    work = [
        Gather(peers, shards[i], zbufs[i], groups[i], homes[i], local.at[i], send.at[i], recv.at[i]) for i in range(6)
    ]

    def swap(b):
        return Swap(
            peers, lambda to: x1_ref.at[b, rows_at(to * part, part)], land_ref.at[b // per, z * per + lax.rem(b, per)],
            xlocal.at[b], xsend.at[b], xrecv.at[b],
        )

    def kept(i):
        return pltpu.make_async_copy(homes[i], fulls[i], keep.at[i])

    def event(name):
        stage, i = name.split()
        getattr(work[int(i)], "step" + stage)()

    @pl.when(step == 0)
    def _():
        held[0] = vec_ref[...]
        enter(peers)
        vec.start(0)
        for w in work:
            w.step0()
        at = 0
        for k, name in enumerate(BEFORE[0]):
            event(name)
            if k % 2 and at < 4:
                vec.finish(at)
                if at < 3:
                    vec.start(at + 1)
                at += 1
        vec_out[...] = held[4].astype(F32)
        kept(0).start()
        kept(1).start()

    for k in (1, 3, 5, 7):

        @pl.when(step == k)
        def _(k=k):
            for name in BEFORE[k]:
                event(name)

    x1_ref[step] = space_rows(
        x_ref[0].astype(F32), vec_out, wqkv_ref, wo_ref, a_ref, qkv_ref, pt_ref.at[0], o_ref
    )
    swap(step).start()

    @pl.when(step == blocks - 1)
    def _():
        for name in AFTER:
            event(name)
        kept(0).wait()
        kept(1).wait()
        vec.drain()
        for w in work:
            w.drain()

        def finish(b, _):
            swap(b).arrive()
            swap(b).drain()
            return 0

        lax.fori_loop(0, blocks, finish, 0)


def first(x, vec, shards, clips):
    blocks, rows, width = x.shape
    tok = blocks * rows
    frames = blocks // clips
    dma = pltpu.SemaphoreType.DMA
    seq = pl.BlockSpec((1, rows, width), lambda b: (b, 0, 0))
    fixed = pl.BlockSpec((VEC_ROWS, width), lambda b: (0, 0))
    out = pl.pallas_call(
        first_kernel,
        grid=(blocks,),
        in_specs=[seq, whole(vec.shape)] + [ANYWHERE] * 6,
        out_specs=[rows_spec(rows, width), rows_spec(rows, 3 * width), probs_spec(rows), rows_spec(rows, width), ANYWHERE]
        + [ANYWHERE] * 6 + [fixed],
        out_shape=[
            sds(tok, width), sds(tok, 3 * width), sds(blocks, HEADS // 2, 2 * rows, rows), sds(tok, width),
            sds(clips, 4 * frames, rows // 4, width),
        ] + [sds(32 * s.shape[0], s.shape[1]) for s in shards] + [sds(VEC_ROWS, width, dtype=F32)],
        scratch_shapes=[
            pltpu.VMEM((width, 3 * width), BF16), pltpu.VMEM((width, width), BF16), pltpu.VMEM((blocks, rows, width), BF16)
        ]
        + [pltpu.VMEM((4, *s.shape), BF16) for s in shards]
        + [pltpu.VMEM((4 * s.shape[0], s.shape[1]), BF16) for s in shards]
        + [
            pltpu.VMEM((5, *vec.shape), BF16), pltpu.VMEM((6, *vec.shape), BF16), dma((6, 2)), dma((6, 16)), dma((6, 16)),
            dma((6,)), dma((6,)), dma((2,)), dma((blocks,)), dma((blocks, 3)), dma((blocks, 3)),
        ],
        compiler_params=params(0),
        name="first",
    )(x, vec.astype(BF16), *shards)
    return out[:4], out[4], out[5:11], out[11]


def middle_kernel(x1_ref, cot_ref, vec_ref, wqkv_ref, wo_ref, win_ref, wout_ref, *refs):
    out_ref, home_ref, g_ref = refs[:3]
    rest = refs[3:11]
    sum_ref = rest[7]
    qkv_ref, pt_ref, gland, dx1_ref, glocal, gsend, grecv, xlocal, xsend, xrecv = refs[11:]
    step = pl.program_id(0)
    blocks, frames, part, width = gland.shape
    rows = frames * part
    clips, per, places, _ = cot_ref.shape
    chunks = blocks // clips
    mine = places // 4
    z = lax.axis_index("seq")
    peers = partners()

    def swap_in(b):
        clip, chunk = b // chunks, b % chunks
        return Swap(
            peers, lambda to: cot_ref.at[clip, :, rows_at(to * mine + chunk * part, part)],
            gland.at[b, pl.ds(z * per, per)], glocal.at[b], gsend.at[b], grecv.at[b],
        )

    def swap_out(b):
        clip, chunk = b // chunks, b % chunks
        return Swap(
            peers, lambda to: dx1_ref.at[b, pl.ds(to * per, per)],
            home_ref.at[clip, :, rows_at(z * mine + chunk * part, part)], xlocal.at[b], xsend.at[b], xrecv.at[b],
        )

    @pl.when(step == 0)
    def _():
        sum_ref[...] = jnp.zeros_like(sum_ref)
        enter({k: v for k, v in peers.items() if k[0] == "z"})

        def begin(b, _):
            swap_in(b).start()
            return 0

        lax.fori_loop(0, blocks, begin, 0)

    swap_in(step).arrive()
    g16 = gland[step].reshape(rows, width)
    g_ref[...] = g16
    x1 = x1_ref[0].reshape(rows, width).astype(F32)
    out, dx1 = place_rows(x1, g16, part, vec_ref, wqkv_ref, wo_ref, win_ref, wout_ref, *rest, qkv_ref, pt_ref)
    out_ref[0] = out.reshape(frames, part, width)
    dx1_ref[step] = dx1.reshape(frames, part, width)
    swap_out(step).start()

    @pl.when(step == blocks - 1)
    def _():
        def finish(b, _):
            swap_in(b).drain()
            swap_out(b).arrive()
            swap_out(b).drain()
            return 0

        lax.fori_loop(0, blocks, finish, 0)


def middle(x1, cot, vec, wqkv, wo, win, wout):
    clips, frames, mine, width = x1.shape
    rows = 256
    part = rows // frames
    per = mine // part
    blocks = clips * per
    tok = blocks * rows
    ff = win.shape[1]
    dma = pltpu.SemaphoreType.DMA
    n = rows_spec(rows, width)
    return pl.pallas_call(
        middle_kernel,
        grid=(blocks,),
        in_specs=[pl.BlockSpec((1, frames, part, width), lambda b: (b // per, 0, b % per, 0)), ANYWHERE]
        + [whole(w.shape) for w in (vec, wqkv, wo, win, wout)],
        out_specs=[
            pl.BlockSpec((1, frames, part, width), lambda b: (b, 0, 0, 0)), ANYWHERE, n, n, rows_spec(rows, 3 * width), n, n,
            n, rows_spec(rows, ff), rows_spec(rows, ff), pl.BlockSpec((SUM_ROWS, 8, width), lambda b: (0, 0, 0)),
        ],
        out_shape=[
            sds(blocks, frames, part, width), sds(*cot.shape), sds(tok, width), sds(tok, width), sds(tok, 3 * width),
            sds(tok, width), sds(tok, width), sds(tok, width), sds(tok, ff), sds(tok, ff),
            sds(SUM_ROWS, 8, width, dtype=F32),
        ],
        scratch_shapes=[
            pltpu.VMEM((rows, 3 * width), BF16), pltpu.VMEM((HEADS // 2, 2 * rows, rows), BF16),
            pltpu.VMEM((blocks, frames, part, width), BF16), pltpu.VMEM((blocks, frames, part, width), BF16),
            dma((blocks,)), dma((blocks, 3)), dma((blocks, 3)), dma((blocks,)), dma((blocks, 3)), dma((blocks, 3)),
        ],
        compiler_params=params(1),
        name="middle",
    )(x1, cot, vec, wqkv, wo, win, wout)


class Scatter:
    def __init__(self, peers, unit, piece, core, first, second, zsend, zgot, out, send, recv):
        self.peers, self.unit, self.piece, self.core = peers, unit, piece, core
        self.first, self.second, self.zsend, self.zgot, self.out = first, second, zsend, zgot, out
        self.send, self.recv = send, recv
        self.rows = core.shape[1]

    def block(self, i, c):
        return rows_at((2 * i + c) * self.rows, self.rows)

    def copy(self, i):
        y, x, c, z = position()
        along_x = self.unit % 2 == 0
        if i < 4:
            src, dst, kind = self.piece.at[self.block(i, 1 - c)], self.core.at[i], "core"
        elif i < 6:
            k = i - 4
            src = self.core.at[2 * k + 1 - x] if along_x else self.core.at[2 * (1 - y) + k]
            dst, kind = self.first.at[k], "x" if along_x else "y"
        elif i == 6:
            src, dst = self.first.at[1 - y if along_x else 1 - x], self.second
            kind = "y" if along_x else "x"
        else:
            j = i - 6
            src, dst, kind = self.zsend.at[lax.rem(z + j, 4)], self.zgot.at[j - 1], f"z{j}"
        return pltpu.make_async_remote_copy(
            src_ref=src, dst_ref=dst, send_sem=self.send.at[i], recv_sem=self.recv.at[i], device_id=self.peers[kind],
            device_id_type=MESH,
        )

    def start(self, items):
        for i in items:
            self.copy(i).start()

    def arrive(self, items):
        for i in items:
            self.copy(i).wait_recv()

    def sent(self, items):
        for i in items:
            self.copy(i).wait_send()

    def step0(self):
        self.start(range(4))

    def step1(self):
        _, _, c, _ = position()
        self.arrive(range(4))

        def add(i, _):
            self.core[i] = (self.piece[self.block(i, c)].astype(F32) + self.core[i].astype(F32)).astype(BF16)
            return 0

        lax.fori_loop(0, 4, add, 0)
        self.start((4, 5))
        self.sent(range(4))

    def step2(self):
        y, x, _, _ = position()
        self.arrive((4, 5))
        for i in range(2):
            own = self.core[2 * i + x] if self.unit % 2 == 0 else self.core[2 * y + i]
            self.first[i] = (self.first[i].astype(F32) + own.astype(F32)).astype(BF16)
        self.start((6,))

    def step3(self):
        y, x, _, _ = position()
        self.arrive((6,))
        r = self.zsend.shape[1]
        total = self.first[y if self.unit % 2 == 0 else x].astype(F32) + self.second[...].astype(F32)
        for i in range(4):
            self.zsend[i] = total[i * r : (i + 1) * r].astype(BF16)
        self.start((7, 8, 9))

    def step4(self):
        self.arrive((7, 8, 9))
        total = self.zsend[lax.axis_index("seq")].astype(F32)
        for i in range(3):
            total = total + self.zgot[i].astype(F32)
        self.out[...] = total

    def drain(self):
        self.sent(range(4, 10))


PANELS, BLOCKS, UNITS, SLOTS = 12, 8, 16, 6
STEPS = PANELS + BLOCKS + UNITS - PANELS
AFTER_STEP = {
    3: ("0 0", "0 1", "0 2", "0 3"), 4: ("1 0", "1 1", "0 4"), 5: ("1 2", "1 3", "0 5"), 6: ("2 0", "2 1", "0 6"), 7: ("0 7",),
    8: ("2 2", "2 3", "3 0", "3 1", "1 4", "1 5", "0 8"), 9: ("4 0", "4 1", "0 9"),
    10: ("3 2", "3 3", "2 4", "2 5", "1 6", "1 7", "0 10"), 11: ("4 2", "4 3", "0 11"),
    12: ("3 4", "3 5", "2 6", "2 7", "1 8", "1 9"), 13: ("4 4", "4 5", "3 6", "3 7", "1 10", "1 11"),
    14: ("2 8", "2 9", "4 6", "4 7"), 16: ("3 8", "3 9", "2 10", "2 11"), 17: ("4 8", "4 9"), 18: ("3 10", "3 11"),
    19: ("4 10", "4 11"), 20: ("0 12",), 21: ("1 12", "0 13"), 22: ("1 13", "2 12", "0 14"), 23: ("2 13", "1 14", "0 15"),
}
TAIL = ("1 15", "3 12", "3 13", "2 14", "2 15", "4 12", "4 13", "3 14", "3 15", "4 14", "4 15")
OUT_AT = (0, 2, 5, 7, 10, 12, 14, 16)


def last_kernel(
    x_ref, g1_ref, qkv_ref, pt_ref, vec_ref, sums_ref, wqkv_ref, wo_ref, z_ref, g_ref, a3_ref, dh_ref, ot_ref, gt_ref, a2_ref,
    dp_ref, a1_ref, o_ref, g1_all, out_ref, dx_ref, sqkv_out, so_out, tqkv_out, to_out, win_out, wout_out, vec_out, home_ref,
    dps_ref, lbuf, rbuf, pieces, core, one, two, zsend, zgot, dpbuf, ssum, held, got, lsem, rsem, send, recv, vsend, vrecv,
    dpsem, olocal, osend, orecv,
):
    step = pl.program_id(0)
    z = lax.axis_index("seq")
    peers = partners()
    width = x_ref.shape[2]
    rows = core.shape[2]
    small = zsend.shape[2]
    blocks, frames, part, _ = out_ref.shape
    clips, per, places, _ = home_ref.shape
    chunks, mine = blocks // clips, places // 4
    vec = Sum(peers, held, got, vsend, vrecv)

    def columns(i):
        return pl.ds(pl.multiple_of(i * width, width), width)

    def out_of(u):
        if u < 4:
            return wout_out.at[pl.ds(u * small, small)]
        if u == 8:
            return to_out
        if u == 12:
            return so_out
        ref, i = (win_out, u - 4) if u < 8 else (tqkv_out, u - 9) if u < 12 else (sqkv_out, u - 13)
        return ref.at[:, pl.ds(i * width, width)]

    work = [
        Scatter(
            peers, u, pieces.at[u % SLOTS], core.at[u], one.at[u], two.at[u], zsend.at[u], zgot.at[u], out_of(u), send.at[u],
            recv.at[u],
        )
        for u in range(UNITS)
    ]

    def event(name):
        stage, u = name.split()
        getattr(work[int(u)], "step" + stage)()

    def swap(b):
        return Swap(
            peers, lambda to: out_ref.at[b, pl.ds(to * per, per)],
            home_ref.at[b // chunks, :, rows_at(z * mine + (b % chunks) * part, part)], olocal.at[b], osend.at[b], orecv.at[b],
        )

    def load(ref, at, buf, sem, slot):
        src = ref if at is None else ref.at[:, columns(at)]
        return pltpu.make_async_copy(src, buf.at[slot], sem.at[slot])

    def fetch(p, left, l_at, right, r_at):
        slot = lax.rem(p, 2)
        load(left, l_at, lbuf, lsem, slot).start()
        load(right, r_at, rbuf, rsem, slot).start()

    def fetch_panel(p):
        for least, most, left, right, which in (
            (0, 4, z_ref, g_ref, "l"), (4, 8, a3_ref, dh_ref, "r"), (8, 9, ot_ref, gt_ref, ""), (9, 12, a2_ref, dp_ref, "r"),
            (12, 13, o_ref, g1_all, ""), (13, 16, a1_ref, dps_ref, "r"),
        ):

            @pl.when((p >= least) & (p < most))
            def _():
                at = p - least
                fetch(p, left, at if which == "l" else None, right, at if which == "r" else None)

    def dp_out(b):
        return pltpu.make_async_copy(dpbuf.at[b % 2], dps_ref.at[rows_at(b * x_ref.shape[1], x_ref.shape[1])], dpsem.at[b % 2])

    is_block = (step >= PANELS) & (step < PANELS + BLOCKS)
    panel = jnp.where(step < PANELS, step, step - BLOCKS)

    @pl.when(step == 0)
    def _():
        ssum[...] = sums_ref[...]
        enter(peers)
        fetch_panel(step)

    for b, at in enumerate(OUT_AT):

        @pl.when(step == at)
        def _(b=b):
            swap(b).start()

    @pl.when((step < PANELS - 1) | (step >= PANELS + BLOCKS - 1) & (step < STEPS - 1))
    def _():
        fetch_panel(jnp.where(step < PANELS, step + 1, step + 1 - BLOCKS))

    @pl.when(jnp.logical_not(is_block))
    def _():
        slot = lax.rem(panel, 2)
        load(z_ref, 0, lbuf, lsem, slot).wait()
        load(z_ref, 0, rbuf, rsem, slot).wait()
        total = outer_sum(lbuf[slot], rbuf[slot])

        @pl.when(panel >= 4)
        def _():
            pieces[lax.rem(panel, SLOTS)] = total.astype(BF16)

        @pl.when(panel < 4)
        def _():
            cut = total.reshape(2, 4, 4, small, width)
            for d in range(2):
                for i in range(4):
                    both = jnp.concatenate([cut[d, k, i] for k in range(4)], axis=0)
                    pieces[i, rows_at((2 * panel + d) * rows, rows)] = both.astype(BF16)

    @pl.when(is_block)
    def _():
        b = step - PANELS

        @pl.when(b >= 2)
        def _():
            dp_out(b - 2).wait()

        dx_ref[0] = space_back_rows(
            x_ref[0].astype(F32), g1_ref[0], qkv_ref, pt_ref.at[0], vec_ref, wqkv_ref, wo_ref, dpbuf.at[lax.rem(b, 2)], ssum
        )
        dp_out(b).start()

    @pl.when(step == PANELS + BLOCKS - 1)
    def _():
        dp_out(step - PANELS - 1).wait()
        dp_out(step - PANELS).wait()
        held[0] = jnp.concatenate([jnp.sum(ssum[i], axis=0, keepdims=True) for i in range(SUM_ROWS)], axis=0)
        vec.start(0)

    for k, names in AFTER_STEP.items():

        @pl.when(step == k)
        def _(k=k, names=names):
            for name in names:
                event(name)
            if k >= PANELS + BLOCKS:
                level = k - PANELS - BLOCKS
                vec.finish(level)
                if level < 3:
                    vec.start(level + 1)

    @pl.when(step == STEPS - 1)
    def _():
        for name in TAIL:
            event(name)
        vec_out[...] = held[4]
        vec.drain()
        for w in work:
            w.drain()

        def finish(b, _):
            swap(b).arrive()
            swap(b).drain()
            return 0

        lax.fori_loop(0, blocks, finish, 0)


def last(x, g1, home, saved, vec, wqkv, wo, out, shapes):
    z, g, a3, dh, ot, gt, a2, dp, a1, o, qkv, pt, sums = saved
    blocks, rows, width = x.shape
    tok = blocks * rows
    dma = pltpu.SemaphoreType.DMA
    in_vmem = pl.BlockSpec(memory_space=pltpu.VMEM)

    def at(s):
        return jnp.minimum(jnp.maximum(s - PANELS, 0), BLOCKS - 1)

    seq = pl.BlockSpec((1, rows, width), lambda s: (at(s), 0, 0))
    small = width // 32
    result = pl.pallas_call(
        last_kernel,
        grid=(STEPS,),
        in_specs=[
            seq, seq, pl.BlockSpec((rows, 3 * width), lambda s: (at(s), 0)),
            pl.BlockSpec((1, HEADS // 2, 2 * rows, rows), lambda s: (at(s), 0, 0, 0)),
        ] + [whole(v.shape) for v in (vec, sums, wqkv, wo)] + [ANYWHERE] * 12,
        out_specs=[seq] + [in_vmem] * 7 + [ANYWHERE] * 2,
        out_shape=[sds(*x.shape)] + [sds(*s, dtype=F32) for s in shapes]
        + [sds(SUM_ROWS, width, dtype=F32), sds(*home), sds(tok, 3 * width)],
        scratch_shapes=[
            pltpu.VMEM((2, tok, width), BF16), pltpu.VMEM((2, tok, width), BF16), pltpu.VMEM((SLOTS, width, width), BF16),
            pltpu.VMEM((UNITS, 4, 4 * small, width), BF16), pltpu.VMEM((UNITS, 2, 4 * small, width), BF16),
            pltpu.VMEM((UNITS, 4 * small, width), BF16), pltpu.VMEM((UNITS, 4, small, width), BF16),
            pltpu.VMEM((UNITS, 3, small, width), BF16), pltpu.VMEM((2, rows, 3 * width), BF16),
            pltpu.VMEM((SUM_ROWS, 8, width), F32), pltpu.VMEM((5, SUM_ROWS, width), F32), pltpu.VMEM((6, SUM_ROWS, width), F32),
            dma((2,)), dma((2,)), dma((UNITS, 10)), dma((UNITS, 10)), dma((6,)), dma((6,)), dma((2,)), dma((blocks,)),
            dma((blocks, 3)), dma((blocks, 3)),
        ],
        compiler_params=params(2),
        name="last",
    )(x, g1, qkv, pt, vec, sums, wqkv, wo, z, g, a3, dh, ot, gt, a2, dp, a1, o, g1.reshape(tok, width), out)
    return result[0], result[1:7], result[7], result[8]


def ring_layer(inputs, cotangent, shards, vec):
    clips, frames, places, width = inputs.shape
    x = inputs.reshape(clips * frames, places, width)
    (a1, qkv, pt, o), x1, (wqkv, wo, tqkv, to, win, wout), vec = first(x, vec, shards, clips)
    out, g1, g, a2, dp, ot, gt, a3, z, dh, sums = middle(x1, cotangent, vec, tqkv, to, win, wout)
    saved = (z, g, a3, dh, ot, gt, a2, dp, a1, o, qkv, pt, sums)
    dx, grads, rows, output = last(
        x, g1.reshape(x.shape), inputs.shape, saved, vec, wqkv, wo, out, [s.shape for s in shards]
    )
    return output, dx.reshape(inputs.shape), grads, rows


def my_index():
    return lax.axis_index("dp") * lax.axis_size("seq") + lax.axis_index("seq")


def spread_vectors(shards, width):
    devices = lax.axis_size("dp") * lax.axis_size("seq")
    me = my_index()
    rows = []
    for items in (NARROW, WIDE, (LONG,)):
        part = jnp.stack([shards[i] for i in items]).astype(F32)
        size = part.shape[1]
        zero = jnp.zeros((len(items), devices * size), F32)
        rows.append(lax.dynamic_update_slice(zero, part, (0, me * size)).reshape(-1, width))
    rows = jnp.concatenate(rows)
    return jnp.pad(rows, ((0, VEC_ROWS - rows.shape[0]), (0, 0)))


def own_vectors(rows):
    devices = lax.axis_size("dp") * lax.axis_size("seq")
    me = my_index()
    out, at = {}, 0
    width = rows.shape[1]
    for items, height in ((NARROW, 1), (WIDE, 2), ((LONG,), 4)):
        block = rows[at : at + height * len(items)].reshape(len(items), height * width)
        size = height * width // devices
        part = lax.dynamic_slice(block, (0, me * size), (len(items), size))
        for k, item in enumerate(items):
            out[item] = part[k]
        at += height * len(items)
    return [out[i] for i in range(12)]


def on_device(
    ring, inputs, norm_one_gain, norm_one_shift, space_qkv, space_qv_bias, space_out, space_out_bias,
    norm_two_gain, norm_two_shift, time_qkv, time_qv_bias, time_out, time_out_bias,
    norm_three_gain, norm_three_shift, mlp_in, mlp_in_bias, mlp_out, mlp_out_bias, cotangent,
):
    width = inputs.shape[-1]
    vec = spread_vectors(
        (norm_one_gain, norm_one_shift, space_qv_bias, space_out_bias, norm_two_gain, norm_two_shift,
         time_qv_bias, time_out_bias, norm_three_gain, norm_three_shift, mlp_in_bias, mlp_out_bias), width
    )
    shards = (space_qkv, space_out, time_qkv, time_out, mlp_in, mlp_out)
    layer = ring_layer if ring else plain_layer
    output, dx, grads, rows = layer(inputs, cotangent, shards, vec)
    gsqkv, gso, gtqkv, gto, gin, gout = grads
    vecs = own_vectors(rows)
    return (
        output, dx, vecs[0], vecs[1], gsqkv, vecs[2], gso, vecs[3], vecs[4], vecs[5], gtqkv,
        vecs[6], gto, vecs[7], vecs[8], vecs[9], gin, vecs[10], gout, vecs[11],
    )


def solution(mesh):
    tokens = P("dp", "seq", None, None)
    vector, matrix = P(("dp", "seq")), P(("dp", "seq"), None)
    weights = (vector, vector, matrix, vector, matrix, vector) * 3
    ring = mesh.shape["dp"] == 8 and mesh.shape["seq"] == 4
    return jax.shard_map(
        functools.partial(on_device, ring),
        mesh=mesh,
        in_specs=(tokens,) + weights + (tokens,),
        out_specs=(tokens, tokens) + weights,
        check_vma=False,
    )
```

time: 1220 us -> 474 us (0.39)
  Pallas kernels: 0 us -> 455 us
  matrix products: 423 us -> 0 us
  local copies, waits for them, and re-layouts: 280 us -> 15.8 us
  waiting for transfers between devices: 258 us -> 0 us
  other arithmetic: 118 us -> 1.32 us
  blocking collectives: 77.9 us -> 0 us
  starting transfers between devices: 37.6 us -> 0 us
  between operations: 21 us -> 0.77 us
    pallas_call x0 -> x3, Pallas kernels: none -> 455 us  [the longest x1 174 us: last(): pl.pallas_call(last_kernel, grid=(STEPS,), in_specs=[seq, seq, pl.BlockSp...]
    dot_general x60 -> x0, matrix products: 423 us -> none  [the longest x12 107 us: back_dot(): lax.dot_general(grad, weight, (((1,), (1,)), ((), ())), preferred_element...]
    reduce_scatter x12 -> x0, waiting for transfers between devices: 127 us -> none  [the longest x6 95.5 us: on_device(): lax.psum_scatter(as_sent(partial_rows), 'seq', scatter_dimension=0, tiled...]
    all_to_all x8 -> x0, waiting for transfers between devices: 115 us -> none  [the longest x2 42.2 us: forward(): lax.all_to_all(by_frame, 'seq', split_axis=2, concat_axis=1, tiled=True)]
    reshape x18 -> x3, local copies, waits for them, and re-layouts: 97.4 us -> 0.05 us  [the longest x2 0.03 us: spread_vectors(): lax.dynamic_update_slice(zero, part, (0, me * size)).reshape(-1, width)]
    convert_element_type x18 -> x0, local copies, waits for them, and re-layouts: 89.6 us -> none  [the longest x6 53.7 us: attend_back(): jnp.stack([grad_query, grad_keys, grad_values], axis=2).astype(jnp.bfloat16)]
    unnamed x3 -> x0, blocking collectives: 77.9 us -> none
    convert_element_type x53 -> x1, other arithmetic: 64.7 us -> 0.68 us  [spread_vectors(): part = jnp.stack([shards[i] for i in items]).astype(F32)]
  transfers between devices with their start and end apart: 26 -> 0, of which waited for: 13 -> 0; matrix products, arithmetic and copies ran while one was open for 52% -> 0% of each run, Pallas kernels for 0% -> 0%
where the time goes in v1:
time: 474 us; the launch traced here: 473 us
  Pallas kernels  455 us (96%)
  local copies, waits for them, and re-layouts  15.8 us (3%)
    pallas_call x1, Pallas kernels, last(): pl.pallas_call(last_kernel, grid=(STEPS,), in_specs=[seq, seq, pl.BlockSp...  174 us
    pallas_call x1, Pallas kernels, middle(): pl.pallas_call(middle_kernel, grid=(blocks,), in_specs=[pl.BlockSpec((1,...  149 us
    pallas_call x1, Pallas kernels, first(): pl.pallas_call(first_kernel, grid=(blocks,), in_specs=[seq, whole(vec.sha...  133 us
    unnamed x24, local copies, waits for them, and re-layouts  10.5 us

profile of v1, /device:TPU:0, one launch (start us, length us, event | category | flops | bytes accessed | tf_op | source)
XLA Modules:
  0.0 473.4 jit_solution(13691966174215271721)
XLA Ops:
  0.7 1.5 stack.49
  2.1 0.2 dynamic_update_slice.9
  2.3 0.8 dynamic_update_slice.11
  3.2 0.7 maximum_convert_fusion
  3.9 0.2 dynamic_update_slice.10
  4.1 0.6 fusion.4.vec_ref
  4.7 132.9 %first.1 = (bf16[2048,768]{1,0:T(8,128)(2,1)}, bf16[2048,2304]{1,0:T(8,128)(2,1)}, bf16[8,6,512,256]{3,2,1,0:T(8,128)(2,1)}, bf16[2048,768]{1,0:T(8,128)(2,1)}, ...) custom-call(bf16[8,256,768]{2,1,0:T(8,128)(2,1)} %bitcast.49, ...), custom_call_target="tpu_custom_call" | custom-call | tf_op jit(solution)/shard_map/first/pallas_call | solution.py:609
  137.6 148.7 %middle.1 = (bf16[8,16,16,768]{3,2,1,0:T(8,128)(2,1)}, bf16[2,4,256,768]{3,2,1,0:T(8,128)(2,1)}, bf16[2048,768]{1,0:T(8,128)(2,1)}, bf16[2048,768]{1,0:T(8,128)(...) custom-call(bf16[2,16,64,768]{3,2,1,0:T(8,128)(2,1)} %get-tuple-elem, ...), custom_call_target="tpu_custom_call" | custom-call | tf_op jit(solution)/shard_map/middle/pallas_call | solution.py:703
  286.3 173.9 %last.1 = (bf16[8,256,768]{2,1,0:T(8,128)(2,1)}, f32[24,2304]{1,0:T(8,128)}, f32[24,768]{1,0:T(8,128)}, f32[24,2304]{1,0:T(8,128)}, f32[24,768]{1,0:T(8,128)}, /...) custom-call(bf16[8,256,768]{2,1,0:T(8,128)(2,1)} %bitcast.50, ...), custom_call_target="tpu_custom_call" | custom-call | tf_op jit(solution)/shard_map/last/pallas_call | solution.py:996
  460.2 0.8 slice.42
  461.0 0.6 dynamic-slice_bitcast_fusion
  461.6 0.8 slice_bitcast_fusion
  462.5 0.1 constant_dynamic-slice_fusion.2
  462.5 0.5 slice_bitcast_fusion.1
  463.1 0.6 fusion.5
  463.7 3.9 copy.52
  467.6 0.0 copy-done
  467.6 0.0 copy-start.5
  467.6 0.0 copy-start.2
  467.6 0.0 copy-start.1
  467.6 1.7 copy.53
  469.3 0.0 copy-done.4
  469.3 0.7 copy.54
  470.0 0.0 copy-done.6
  470.0 0.6 copy.55
  470.6 0.0 copy-done.3
  470.6 0.7 copy.56
  471.3 0.0 copy-done.5
  471.3 0.6 copy.57
  471.9 0.7 copy.58
  472.7 0.0 copy-done.1
  472.7 0.7 copy.59
  (13 shorter events, 0.1 us)
Async XLA Ops:
  463.7 3.9 copy-start
  467.6 1.7 copy-start.4
  467.6 2.4 copy-start.6
  467.6 3.0 copy-start.3
  467.6 3.7 copy-start.5
  467.6 4.3 copy-start.2
  467.6 5.0 %copy-start.1 = (f32[96,768]{1,0:T(8,128)S(1)}, f32[96,768]{1,0:T(8,128)}, u32[]{:S(2)}) copy-start(f32[96,768]{1,0:T(8,128)} %get-tuple-element.135) | copy-start | bytes 884740

commit v2 on v1

--- a/solution.py
+++ b/solution.py
@@ -110,7 +110,7 @@
 LONG = 10
 VEC_ROWS = 32
 SUM_ROWS = 24
-VMEM_LIMIT = 60 * 2**20
+VMEM_LIMIT = 61 * 2**20
 
 
 def row(vec_ref, i):
@@ -135,7 +135,7 @@
 
 
 def place_rows(
-    x1, g16, period, vec_ref, wqkv_ref, wo_ref, win_ref, wout_ref, a2_ref, dp_ref, o_ref, gt_ref, a3_ref, z_ref, dh_ref,
+    x1, take_g, period, vec_ref, wqkv_ref, wo_ref, win_ref, wout_ref, a2_ref, dp_ref, o_ref, gt_ref, a3_ref, z_ref, dh_ref,
     sum_ref, qkv_ref, pt_ref,
 ):
     rows, width = x1.shape
@@ -149,6 +149,7 @@
     hat3, rstd3 = norm(x2)
     a3 = (hat3 * row(vec_ref, GAIN3) + row(vec_ref, SHIFT3)).astype(BF16)
     a3_ref[...] = a3
+    g16 = take_g()
     g = g16.astype(F32)
     sum_ref[BOUT] += fold(g)
     y = x2 + row(vec_ref, BOUT)
@@ -230,8 +231,11 @@
         sum_ref[...] = jnp.zeros_like(sum_ref)
 
     x1 = x1_ref[0].reshape(rows, width).astype(F32)
-    g16 = g_ref[0].reshape(rows, width)
-    out, dx1 = place_rows(x1, g16, places, vec_ref, wqkv_ref, wo_ref, win_ref, wout_ref, *rest)
+
+    def take_g():
+        return g_ref[0].reshape(rows, width)
+
+    out, dx1 = place_rows(x1, take_g, places, vec_ref, wqkv_ref, wo_ref, win_ref, wout_ref, *rest)
     out_ref[0] = out.reshape(frames, places, width)
     dx1_ref[0] = dx1.reshape(frames, places, width)
 
@@ -353,12 +357,18 @@
     return d // 4, lax.rem(d // 2, 2), lax.rem(d, 2), z
 
 
+def partner(z):
+    return z + 1 - 2 * lax.rem(z, 2)
+
+
 def partners():
     y, x, c, z = position()
     return {
         "x": (4 * y + 2 * (1 - x) + c, z),
         "y": (4 * (1 - y) + 2 * x + c, z),
         "core": (4 * y + 2 * x + 1 - c, z),
+        "pair": (4 * y + 2 * x + c, partner(z)),
+        "across": (4 * y + 2 * x + c, 3 - z),
         "z1": (4 * y + 2 * x + c, lax.rem(z + 1, 4)),
         "z2": (4 * y + 2 * x + c, lax.rem(z + 2, 4)),
         "z3": (4 * y + 2 * x + c, lax.rem(z + 3, 4)),
@@ -367,9 +377,10 @@
 
 def enter(peers):
     barrier = pltpu.get_barrier_semaphore()
-    for peer in peers.values():
+    greeted = [peer for kind, peer in peers.items() if kind not in ("pair", "across")]
+    for peer in greeted:
         pl.semaphore_signal(barrier, inc=1, device_id=peer, device_id_type=MESH)
-    pl.semaphore_wait(barrier, len(peers))
+    pl.semaphore_wait(barrier, len(greeted))
 
 
 class Sum:
@@ -402,34 +413,45 @@
 
 
 class Gather:
-    def __init__(self, peers, shard, zbuf, group, full, local, send, recv):
+    def __init__(self, peers, direct, shard, zbuf, group, full, local, send, recv):
         self.peers, self.shard, self.zbuf, self.group, self.full = peers, shard, zbuf, group, full
         self.local, self.send, self.recv = local, send, recv
+        self.direct = direct
         self.rows, self.cols = group.shape
+        z = lax.axis_index("seq")
+        self.inner = (z == 1) | (z == 2)
 
     def place(self, which, half):
         y, x, c, _ = position()
         y, x = {"own": (y, x), "x": (y, 1 - x), "y": (1 - y, x), "xy": (1 - y, 1 - x)}[which]
         rows = pl.ds(pl.multiple_of((4 * y + 2 * x + c) * self.rows, self.rows), self.rows)
         n = self.cols // 2
-        return (rows, slice(None)) if half is None else (rows, pl.ds(half * n, n))
+        return (rows, pl.ds(0, self.cols)) if half is None else (rows, pl.ds(half * n, n))
 
     PLAN = {
-        3: ("own", 0, "x"), 4: ("own", 1, "y"), 5: ("own", 0, "y"), 6: ("x", 0, "y"), 7: ("own", 1, "x"), 8: ("y", 1, "x"),
-        9: ("own", None, "core"), 10: ("x", 0, "core"), 11: ("y", 1, "core"), 12: ("y", 0, "core"), 13: ("xy", 0, "core"),
-        14: ("x", 1, "core"), 15: ("xy", 1, "core"),
+        5: ("own", 0, "x"), 6: ("own", 1, "y"), 7: ("own", 0, "y"), 8: ("x", 0, "y"), 9: ("own", 1, "x"), 10: ("y", 1, "x"),
+        11: ("own", None, "core"), 12: ("x", 0, "core"), 13: ("y", 1, "core"), 14: ("y", 0, "core"), 15: ("xy", 0, "core"),
+        16: ("x", 1, "core"), 17: ("xy", 1, "core"),
     }
 
     def copy(self, i):
-        if i < 3:
+        if i < 5:
             z = lax.axis_index("seq")
-            src, dst, kind = self.shard, self.zbuf.at[z], ("z1", "z2", "z3")[i]
+            if self.direct:
+                return self.remote(self.shard, self.zbuf.at[z], i, ("z1", "z2", "z3")[i])
+            whose = (z, z, partner(z), 3 - z, partner(3 - z))[i]
+            dst = self.zbuf.at[whose]
+            src = self.shard if i < 2 else dst
+            kind = ("pair", "across", "across", "pair", "pair")[i]
         else:
             which, half, kind = self.PLAN[i]
             at = self.place(which, half)
             src = dst = self.full.at[at]
             if which == "own":
                 src = self.group if half is None else self.group.at[:, pl.ds(half * (self.cols // 2), self.cols // 2)]
+        return self.remote(src, dst, i, kind)
+
+    def remote(self, src, dst, i, kind):
         return pltpu.make_async_remote_copy(
             src_ref=src, dst_ref=dst, send_sem=self.send.at[i], recv_sem=self.recv.at[i], device_id=self.peers[kind],
             device_id_type=MESH,
@@ -451,30 +473,66 @@
 
     def step0(self):
         self.own_in().start()
-        self.start((0, 1, 2))
+        if self.direct:
+            self.start((0, 1, 2))
+            return
+        self.start((0,))
+
+        @pl.when(self.inner)
+        def _():
+            self.start((1,))
+
+    def stepa(self):
+        self.arrive((0,))
+
+        @pl.when(self.inner)
+        def _():
+            self.start((2,))
+
+    def stepb(self):
+        @pl.when(self.inner)
+        def _():
+            self.arrive((1,))
+            self.start((3,))
+            self.arrive((2,))
+            self.start((4,))
 
     def step1(self):
+        if self.direct:
+            self.arrive((0, 1, 2))
+        else:
+
+            @pl.when(jnp.logical_not(self.inner))
+            def _():
+                self.arrive((3, 4))
+
         self.own_in().wait()
-        self.arrive((0, 1, 2))
         self.group[...] = jnp.concatenate([self.zbuf[i].astype(F32) for i in range(4)], axis=0).astype(BF16)
         self.own_out().start()
-        self.start((3, 4, 5, 7, 9))
+        self.start((5, 6, 7, 9, 11))
 
     def step2(self):
-        self.arrive((3, 4))
-        self.start((6, 8, 10, 11))
+        self.arrive((5, 6))
+        self.start((8, 10, 12, 13))
 
     def step3(self):
-        self.arrive((5, 7, 6, 8))
-        self.start((12, 14, 13, 15))
+        self.arrive((7, 9, 8, 10))
+        self.start((14, 16, 15, 17))
 
     def step4(self):
-        self.arrive((9, 10, 11, 12, 14, 13, 15))
+        self.arrive((11, 12, 13, 14, 16, 15, 17))
         self.own_out().wait()
 
     def drain(self):
-        for i in range(16):
+        for i in (*range(3 if self.direct else 1), *range(5, 18)):
             self.copy(i).wait_send()
+        if self.direct:
+            return
+
+        @pl.when(self.inner)
+        def _():
+            for i in range(1, 5):
+                self.copy(i).wait_send()
 
 
 class Swap:
@@ -511,11 +569,19 @@
     return pl.ds(pl.multiple_of(start, size), size)
 
 
+GATHERED = ((0, 0), (0, 1), (0, 2), (1, 0), (2, 0), (2, 1), (2, 2), (3, 0), (4, 0), (4, 1), (4, 2), (4, 3), (5, 0))
 BEFORE = {
-    0: ("1 0", "1 1", "2 0", "2 1", "1 2", "3 0", "3 1", "1 3", "4 0", "4 1"),
-    1: ("2 2", "2 3", "1 4"), 3: ("3 2", "3 3", "1 5"), 5: ("2 4", "4 2", "4 3"), 7: ("2 5", "3 4"),
+    0: ("0 0", "0 1", "0 2", "0 3", "1 0", "1 1", "0 4", "0 5", "2 0", "0 6", "1 2", "0 7", "0 8", "0 9", "2 1", "a 4", "1 3", "a 5", "a 6", "a 7", "3 0", "a 8", "2 2", "a 9", "0 10", "4 0", "0 11", "0 12", "3 1", "b 4", "2 3", "b 5", "b 6", "a 10", "4 1", "b 7", "a 11", "3 2", "b 8", "a 12", "3 3", "1 4", "b 9", "4 2", "4 3"),
+    1: ("2 4", "1 5", "b 10", "b 11", "b 12"),
+    2: ("3 4", "1 6", "2 5"),
+    3: ("4 4", "2 6", "1 7"),
+    4: ("3 5", "3 6", "1 8"),
+    5: ("4 5", "4 6", "2 7", "2 8"),
+    6: ("3 7", "1 9"),
+    7: ("4 7", "3 8", "2 9", "1 10"),
 }
-AFTER = ("3 5", "4 4", "4 5")
+AFTER = ("1 11", "1 12", "4 8", "3 9", "2 10", "2 11", "4 9", "2 12", "3 10", "3 11", "4 10", "4 11", "3 12", "4 12")
+VEC_AT = ("1 0", "1 2", "2 1", "3 1")
 
 
 def first_kernel(x_ref, vec_ref, *refs):
@@ -523,8 +589,9 @@
     a_ref, qkv_ref, pt_ref, o_ref, land_ref = refs[6:11]
     fulls, vec_out = refs[11:17], refs[17]
     wqkv_ref, wo_ref, x1_ref = refs[18:21]
-    zbufs, groups = refs[21:27], refs[27:33]
-    held, got, local, send, recv, vsend, vrecv, keep, xlocal, xsend, xrecv = refs[33:]
+    count = len(GATHERED)
+    zbufs, groups = refs[21 : 21 + count], refs[21 + count : 21 + 2 * count]
+    held, got, local, send, recv, vsend, vrecv, keep, xlocal, xsend, xrecv = refs[21 + 2 * count :]
     step = pl.program_id(0)
     blocks, rows, width = x1_ref.shape
     per = land_ref.shape[1] // 4
@@ -533,9 +600,15 @@
     peers = partners()
     vec = Sum(peers, held, got, vsend, vrecv)
     homes = (wqkv_ref, wo_ref) + tuple(fulls[2:])
-    work = [
-        Gather(peers, shards[i], zbufs[i], groups[i], homes[i], local.at[i], send.at[i], recv.at[i]) for i in range(6)
-    ]
+
+    def piece(u):
+        w, at = GATHERED[u]
+        return (ref.at[:, pl.ds(at * width, width)] for ref in (shards[w], homes[w]))
+
+    work = []
+    for u in range(count):
+        shard, full = piece(u)
+        work.append(Gather(peers, u < 4, shard, zbufs[u], groups[u], full, local.at[u], send.at[u], recv.at[u]))
 
     def swap(b):
         return Swap(
@@ -555,21 +628,18 @@
         held[0] = vec_ref[...]
         enter(peers)
         vec.start(0)
-        for w in work:
-            w.step0()
-        at = 0
         for k, name in enumerate(BEFORE[0]):
             event(name)
-            if k % 2 and at < 4:
-                vec.finish(at)
-                if at < 3:
-                    vec.start(at + 1)
-                at += 1
+            if name in VEC_AT:
+                level = VEC_AT.index(name)
+                vec.finish(level)
+                if level < 3:
+                    vec.start(level + 1)
         vec_out[...] = held[4].astype(F32)
         kept(0).start()
         kept(1).start()
 
-    for k in (1, 3, 5, 7):
+    for k in range(1, 8):
 
         @pl.when(step == k)
         def _(k=k):
@@ -603,6 +673,7 @@
     blocks, rows, width = x.shape
     tok = blocks * rows
     frames = blocks // clips
+    count = len(GATHERED)
     dma = pltpu.SemaphoreType.DMA
     seq = pl.BlockSpec((1, rows, width), lambda b: (b, 0, 0))
     fixed = pl.BlockSpec((VEC_ROWS, width), lambda b: (0, 0))
@@ -619,10 +690,11 @@
         scratch_shapes=[
             pltpu.VMEM((width, 3 * width), BF16), pltpu.VMEM((width, width), BF16), pltpu.VMEM((blocks, rows, width), BF16)
         ]
-        + [pltpu.VMEM((4, *s.shape), BF16) for s in shards]
-        + [pltpu.VMEM((4 * s.shape[0], s.shape[1]), BF16) for s in shards]
+        + [pltpu.VMEM((4, shards[w].shape[0], width), BF16) for w, _ in GATHERED]
+        + [pltpu.VMEM((4 * shards[w].shape[0], width), BF16) for w, _ in GATHERED]
         + [
-            pltpu.VMEM((5, *vec.shape), BF16), pltpu.VMEM((6, *vec.shape), BF16), dma((6, 2)), dma((6, 16)), dma((6, 16)),
+            pltpu.VMEM((5, *vec.shape), BF16), pltpu.VMEM((6, *vec.shape), BF16), dma((count, 2)), dma((count, 18)),
+            dma((count, 18)),
             dma((6,)), dma((6,)), dma((2,)), dma((blocks,)), dma((blocks, 3)), dma((blocks, 3)),
         ],
         compiler_params=params(0),
@@ -632,10 +704,10 @@
 
 
 def middle_kernel(x1_ref, cot_ref, vec_ref, wqkv_ref, wo_ref, win_ref, wout_ref, *refs):
-    out_ref, home_ref, g_ref = refs[:3]
-    rest = refs[3:11]
+    out_ref, home_ref, rest_ref, g_ref = refs[:4]
+    rest = refs[4:12]
     sum_ref = rest[7]
-    qkv_ref, pt_ref, gland, dx1_ref, glocal, gsend, grecv, xlocal, xsend, xrecv = refs[11:]
+    qkv_ref, pt_ref, gland, dx1_ref, glocal, gsend, grecv, xlocal, xsend, xrecv = refs[12:]
     step = pl.program_id(0)
     blocks, frames, part, width = gland.shape
     rows = frames * part
@@ -670,24 +742,35 @@
 
         lax.fori_loop(0, blocks, begin, 0)
 
-    swap_in(step).arrive()
-    g16 = gland[step].reshape(rows, width)
-    g_ref[...] = g16
+    def take_g():
+        swap_in(step).arrive()
+        g16 = gland[step].reshape(rows, width)
+        g_ref[...] = g16
+        return g16
+
     x1 = x1_ref[0].reshape(rows, width).astype(F32)
-    out, dx1 = place_rows(x1, g16, part, vec_ref, wqkv_ref, wo_ref, win_ref, wout_ref, *rest, qkv_ref, pt_ref)
+    out, dx1 = place_rows(x1, take_g, part, vec_ref, wqkv_ref, wo_ref, win_ref, wout_ref, *rest, qkv_ref, pt_ref)
     out_ref[0] = out.reshape(frames, part, width)
     dx1_ref[step] = dx1.reshape(frames, part, width)
-    swap_out(step).start()
+
+    @pl.when(step < blocks - 1)
+    def _():
+        swap_out(step).start()
 
     @pl.when(step == blocks - 1)
     def _():
+        rest_out = pltpu.make_async_copy(dx1_ref.at[blocks - 1], rest_ref, xlocal.at[blocks - 1])
+        rest_out.start()
+
         def finish(b, _):
             swap_in(b).drain()
             swap_out(b).arrive()
             swap_out(b).drain()
             return 0
 
-        lax.fori_loop(0, blocks, finish, 0)
+        lax.fori_loop(0, blocks - 1, finish, 0)
+        swap_in(blocks - 1).drain()
+        rest_out.wait()
 
 
 def middle(x1, cot, vec, wqkv, wo, win, wout):
@@ -706,11 +789,11 @@
         in_specs=[pl.BlockSpec((1, frames, part, width), lambda b: (b // per, 0, b % per, 0)), ANYWHERE]
         + [whole(w.shape) for w in (vec, wqkv, wo, win, wout)],
         out_specs=[
-            pl.BlockSpec((1, frames, part, width), lambda b: (b, 0, 0, 0)), ANYWHERE, n, n, rows_spec(rows, 3 * width), n, n,
-            n, rows_spec(rows, ff), rows_spec(rows, ff), pl.BlockSpec((SUM_ROWS, 8, width), lambda b: (0, 0, 0)),
+            pl.BlockSpec((1, frames, part, width), lambda b: (b, 0, 0, 0)), ANYWHERE, ANYWHERE, n, n,
+            rows_spec(rows, 3 * width), n, n, n, rows_spec(rows, ff), rows_spec(rows, ff), pl.BlockSpec((SUM_ROWS, 8, width), lambda b: (0, 0, 0)),
         ],
         out_shape=[
-            sds(blocks, frames, part, width), sds(*cot.shape), sds(tok, width), sds(tok, width), sds(tok, 3 * width),
+            sds(blocks, frames, part, width), sds(*cot.shape), sds(frames, part, width), sds(tok, width), sds(tok, width), sds(tok, 3 * width),
             sds(tok, width), sds(tok, width), sds(tok, width), sds(tok, ff), sds(tok, ff),
             sds(SUM_ROWS, 8, width, dtype=F32),
         ],
@@ -725,30 +808,38 @@
 
 
 class Scatter:
-    def __init__(self, peers, unit, piece, core, first, second, zsend, zgot, out, send, recv):
-        self.peers, self.unit, self.piece, self.core = peers, unit, piece, core
+    def __init__(self, peers, direct, piece, core, first, second, zsend, zgot, out, send, recv):
+        self.peers, self.piece, self.core = peers, piece, core
         self.first, self.second, self.zsend, self.zgot, self.out = first, second, zsend, zgot, out
         self.send, self.recv = send, recv
-        self.rows = core.shape[1]
+        self.direct = direct
+        z = lax.axis_index("seq")
+        self.inner = (z == 1) | (z == 2)
+        self.rows, self.half = core.shape[1], core.shape[2] // 2
 
     def block(self, i, c):
         return rows_at((2 * i + c) * self.rows, self.rows)
 
     def copy(self, i):
         y, x, c, z = position()
-        along_x = self.unit % 2 == 0
         if i < 4:
             src, dst, kind = self.piece.at[self.block(i, 1 - c)], self.core.at[i], "core"
         elif i < 6:
-            k = i - 4
-            src = self.core.at[2 * k + 1 - x] if along_x else self.core.at[2 * (1 - y) + k]
-            dst, kind = self.first.at[k], "x" if along_x else "y"
-        elif i == 6:
-            src, dst = self.first.at[1 - y if along_x else 1 - x], self.second
-            kind = "y" if along_x else "x"
+            src, dst, kind = self.core.at[2 * (i - 4) + 1 - x, :, pl.ds(0, self.half)], self.first.at[0, i - 4], "x"
+        elif i < 8:
+            src, dst, kind = self.core.at[2 * (1 - y) + i - 6, :, pl.ds(self.half, self.half)], self.first.at[1, i - 6], "y"
+        elif i == 8:
+            src, dst, kind = self.first.at[0, 1 - y], self.second.at[0], "y"
+        elif i == 9:
+            src, dst, kind = self.first.at[1, 1 - x], self.second.at[1], "x"
+        elif self.direct:
+            j = i - 9
+            src, dst, kind = self.zsend.at[lax.rem(z + j, 4)], self.zgot.at[j - 1], f"z{j}"
         else:
-            j = i - 6
-            src, dst, kind = self.zsend.at[lax.rem(z + j, 4)], self.zgot.at[j - 1], f"z{j}"
+            near, far = partner(z), 3 - partner(z)
+            whose = (near, far, partner(far), 3 - z, partner(3 - z), near)[i - 10]
+            src, dst = self.zsend.at[whose], self.zgot.at[(0, 1, 2, 3, 4, 0)[i - 10]]
+            kind = "across" if i in (13, 14) else "pair"
         return pltpu.make_async_remote_copy(
             src_ref=src, dst_ref=dst, send_sem=self.send.at[i], recv_sem=self.recv.at[i], device_id=self.peers[kind],
             device_id_type=MESH,
@@ -774,60 +865,117 @@
         self.arrive(range(4))
 
         def add(i, _):
-            self.core[i] = (self.piece[self.block(i, c)].astype(F32) + self.core[i].astype(F32)).astype(BF16)
+            self.core[i] = self.piece[self.block(i, c)] + self.core[i]
             return 0
 
         lax.fori_loop(0, 4, add, 0)
-        self.start((4, 5))
+        self.start(range(4, 8))
         self.sent(range(4))
 
     def step2(self):
         y, x, _, _ = position()
-        self.arrive((4, 5))
+        n = self.half
+        self.arrive(range(4, 8))
         for i in range(2):
-            own = self.core[2 * i + x] if self.unit % 2 == 0 else self.core[2 * y + i]
-            self.first[i] = (self.first[i].astype(F32) + own.astype(F32)).astype(BF16)
-        self.start((6,))
+            self.first[0, i] = self.first[0, i] + self.core[2 * i + x, :, :n]
+            self.first[1, i] = self.first[1, i] + self.core[2 * y + i, :, n:]
+        self.start((8, 9))
 
     def step3(self):
         y, x, _, _ = position()
-        self.arrive((6,))
+        self.arrive((8, 9))
         r = self.zsend.shape[1]
-        total = self.first[y if self.unit % 2 == 0 else x].astype(F32) + self.second[...].astype(F32)
-        for i in range(4):
-            self.zsend[i] = total[i * r : (i + 1) * r].astype(BF16)
-        self.start((7, 8, 9))
+        for k, at in ((0, y), (1, x)):
+            total = self.first[k, at].astype(F32) + self.second[k].astype(F32)
+            for i in range(4):
+                self.zsend[i, :, k * self.half : (k + 1) * self.half] = total[i * r : (i + 1) * r].astype(BF16)
+        if self.direct:
+            self.start((10, 11, 12))
+            return
+
+        @pl.when(jnp.logical_not(self.inner))
+        def _():
+            self.start((10, 11, 12))
+
+    def stepb(self):
+        @pl.when(self.inner)
+        def _():
+            z = lax.axis_index("seq")
+            self.arrive((10, 11, 12))
+            for whose, i in ((3 - z, 1), (partner(3 - z), 2)):
+                self.zsend[whose] = self.zsend[whose] + self.zgot[i]
+            self.start((13, 14))
+
+    def stepc(self):
+        @pl.when(self.inner)
+        def _():
+            z = lax.axis_index("seq")
+            self.arrive((13, 14))
+            near = partner(z)
+            self.zsend[near] = self.zsend[near] + self.zgot[4]
+            self.start((15,))
 
     def step4(self):
-        self.arrive((7, 8, 9))
-        total = self.zsend[lax.axis_index("seq")].astype(F32)
-        for i in range(3):
-            total = total + self.zgot[i].astype(F32)
-        self.out[...] = total
+        z = lax.axis_index("seq")
+        if self.direct:
+            self.arrive((10, 11, 12))
+            total = self.zsend[z].astype(F32)
+            for i in range(3):
+                total = total + self.zgot[i].astype(F32)
+            self.out[...] = total
+            self.sent((10, 11, 12))
+            return
+
+        @pl.when(self.inner)
+        def _():
+            self.out[...] = self.zsend[z].astype(F32) + self.zgot[0].astype(F32) + self.zgot[3].astype(F32)
+            self.sent((13, 14, 15))
+
+        @pl.when(jnp.logical_not(self.inner))
+        def _():
+            self.arrive((15,))
+            self.out[...] = self.zsend[z].astype(F32) + self.zgot[0].astype(F32)
+            self.sent((10, 11, 12))
 
     def drain(self):
         self.sent(range(4, 10))
 
 
-PANELS, BLOCKS, UNITS, SLOTS = 12, 8, 16, 6
+PANELS, BLOCKS, UNITS, SLOTS = 11, 8, 16, 6
+CHAINED = 12
 STEPS = PANELS + BLOCKS + UNITS - PANELS
 AFTER_STEP = {
-    3: ("0 0", "0 1", "0 2", "0 3"), 4: ("1 0", "1 1", "0 4"), 5: ("1 2", "1 3", "0 5"), 6: ("2 0", "2 1", "0 6"), 7: ("0 7",),
-    8: ("2 2", "2 3", "3 0", "3 1", "1 4", "1 5", "0 8"), 9: ("4 0", "4 1", "0 9"),
-    10: ("3 2", "3 3", "2 4", "2 5", "1 6", "1 7", "0 10"), 11: ("4 2", "4 3", "0 11"),
-    12: ("3 4", "3 5", "2 6", "2 7", "1 8", "1 9"), 13: ("4 4", "4 5", "3 6", "3 7", "1 10", "1 11"),
-    14: ("2 8", "2 9", "4 6", "4 7"), 16: ("3 8", "3 9", "2 10", "2 11"), 17: ("4 8", "4 9"), 18: ("3 10", "3 11"),
-    19: ("4 10", "4 11"), 20: ("0 12",), 21: ("1 12", "0 13"), 22: ("1 13", "2 12", "0 14"), 23: ("2 13", "1 14", "0 15"),
+    3: ("0 0", "0 1", "0 2", "0 3"),
+    4: ("0 4",),
+    5: ("0 5", "1 0", "1 1"),
+    6: ("0 6", "1 2"),
+    7: ("0 7", "1 3", "1 4", "2 0"),
+    8: ("0 8", "2 1"),
+    9: ("0 9", "2 2", "1 5"),
+    10: ("0 10", "2 3", "2 4"),
+    11: ("1 6", "1 7", "3 0", "3 1", "3 2"),
+    12: ("2 5", "1 8", "1 9", "3 3", "3 4", "2 6", "b 0"),
+    13: ("2 7", "1 10", "b 1", "b 2", "3 5"),
+    14: ("2 8", "2 9", "c 0", "3 6"),
+    15: ("2 10", "b 3", "b 4", "c 1", "3 7"),
+    16: ("c 2",),
+    17: ("b 5",),
+    18: ("b 6", "4 0", "3 8"),
+    19: ("0 11", "c 3", "c 4"),
+    20: ("0 12", "b 7", "c 5", "c 6", "4 1", "1 11", "3 9"),
+    21: ("0 13", "1 12", "b 8", "c 7", "4 2", "3 10"),
+    22: ("0 14", "2 11", "1 13", "b 9", "c 8", "4 3", "4 4", "4 5", "4 6", "2 12", "b 10"),
+    23: ("0 15", "1 14", "c 9", "3 11", "4 7", "c 10"),
 }
-TAIL = ("1 15", "3 12", "3 13", "2 14", "2 15", "4 12", "4 13", "3 14", "3 15", "4 14", "4 15")
-OUT_AT = (0, 2, 5, 7, 10, 12, 14, 16)
+TAIL = ("4 8", "2 13", "3 12", "1 15", "4 9", "b 11", "2 14", "4 10", "3 13", "4 12", "c 11", "2 15", "3 14", "4 11", "4 13", "3 15", "4 14", "4 15")
+OUT_AT = (0, 3, 6, 9, 12, 13, 14, 15)
 
 
 def last_kernel(
     x_ref, g1_ref, qkv_ref, pt_ref, vec_ref, sums_ref, wqkv_ref, wo_ref, z_ref, g_ref, a3_ref, dh_ref, ot_ref, gt_ref, a2_ref,
-    dp_ref, a1_ref, o_ref, g1_all, out_ref, dx_ref, sqkv_out, so_out, tqkv_out, to_out, win_out, wout_out, vec_out, home_ref,
-    dps_ref, lbuf, rbuf, pieces, core, one, two, zsend, zgot, dpbuf, ssum, held, got, lsem, rsem, send, recv, vsend, vrecv,
-    dpsem, olocal, osend, orecv,
+    dp_ref, a1_ref, o_ref, rest_ref, out_ref, dx_ref, sqkv_out, so_out, tqkv_out, to_out, win_out, wout_out, vec_out, home_ref,
+    dps_ref, g1_all, lbuf, rbuf, pieces, core, one, two, zsend, zgot, dpbuf, gbuf, gland, ssum, held, got, lsem, rsem, send, recv, vsend, vrecv,
+    dpsem, gsem, olocal, osend, orecv, rlocal, rsend, rrecv,
 ):
     step = pl.program_id(0)
     z = lax.axis_index("seq")
@@ -855,7 +1003,7 @@
 
     work = [
         Scatter(
-            peers, u, pieces.at[u % SLOTS], core.at[u], one.at[u], two.at[u], zsend.at[u], zgot.at[u], out_of(u), send.at[u],
+            peers, u >= CHAINED, pieces.at[u % SLOTS], core.at[u], one.at[u], two.at[u], zsend.at[u % 8], zgot.at[u], out_of(u), send.at[u],
             recv.at[u],
         )
         for u in range(UNITS)
@@ -871,6 +1019,10 @@
             home_ref.at[b // chunks, :, rows_at(z * mine + (b % chunks) * part, part)], olocal.at[b], osend.at[b], orecv.at[b],
         )
 
+    rest = Swap(
+        peers, lambda to: rest_ref.at[pl.ds(to * per, per)], gland.at[:, z], rlocal, rsend, rrecv,
+    )
+
     def load(ref, at, buf, sem, slot):
         src = ref if at is None else ref.at[:, columns(at)]
         return pltpu.make_async_copy(src, buf.at[slot], sem.at[slot])
@@ -894,14 +1046,18 @@
     def dp_out(b):
         return pltpu.make_async_copy(dpbuf.at[b % 2], dps_ref.at[rows_at(b * x_ref.shape[1], x_ref.shape[1])], dpsem.at[b % 2])
 
+    def g1_out(b):
+        return pltpu.make_async_copy(gbuf.at[b % 2], g1_all.at[rows_at(b * x_ref.shape[1], x_ref.shape[1])], gsem.at[b % 2])
+
     is_block = (step >= PANELS) & (step < PANELS + BLOCKS)
     panel = jnp.where(step < PANELS, step, step - BLOCKS)
 
     @pl.when(step == 0)
     def _():
         ssum[...] = sums_ref[...]
+        fetch_panel(step)
         enter(peers)
-        fetch_panel(step)
+        rest.start()
 
     for b, at in enumerate(OUT_AT):
 
@@ -939,9 +1095,23 @@
         @pl.when(b >= 2)
         def _():
             dp_out(b - 2).wait()
-
+            g1_out(b - 2).wait()
+
+        slot = lax.rem(b, 2)
+        gbuf[slot] = g1_ref[0]
+
+        @pl.when(b == BLOCKS - per)
+        def _():
+            rest.arrive()
+
+        @pl.when(b >= BLOCKS - per)
+        def _():
+            for k in range(4):
+                gbuf[slot, pl.ds(k * mine + mine - part, part)] = gland[b - (BLOCKS - per), k]
+
+        g1_out(b).start()
         dx_ref[0] = space_back_rows(
-            x_ref[0].astype(F32), g1_ref[0], qkv_ref, pt_ref.at[0], vec_ref, wqkv_ref, wo_ref, dpbuf.at[lax.rem(b, 2)], ssum
+            x_ref[0].astype(F32), gbuf[slot], qkv_ref, pt_ref.at[0], vec_ref, wqkv_ref, wo_ref, dpbuf.at[lax.rem(b, 2)], ssum
         )
         dp_out(b).start()
 
@@ -949,6 +1119,8 @@
     def _():
         dp_out(step - PANELS - 1).wait()
         dp_out(step - PANELS).wait()
+        g1_out(step - PANELS - 1).wait()
+        g1_out(step - PANELS).wait()
         held[0] = jnp.concatenate([jnp.sum(ssum[i], axis=0, keepdims=True) for i in range(SUM_ROWS)], axis=0)
         vec.start(0)
 
@@ -960,7 +1132,8 @@
                 event(name)
             if k >= PANELS + BLOCKS:
                 level = k - PANELS - BLOCKS
-                vec.finish(level)
+                if level < 4:
+                    vec.finish(level)
                 if level < 3:
                     vec.start(level + 1)
 
@@ -970,6 +1143,7 @@
             event(name)
         vec_out[...] = held[4]
         vec.drain()
+        rest.drain()
         for w in work:
             w.drain()
 
@@ -981,7 +1155,7 @@
         lax.fori_loop(0, blocks, finish, 0)
 
 
-def last(x, g1, home, saved, vec, wqkv, wo, out, shapes):
+def last(x, g1, rest, home, saved, vec, wqkv, wo, out, shapes):
     z, g, a3, dh, ot, gt, a2, dp, a1, o, qkv, pt, sums = saved
     blocks, rows, width = x.shape
     tok = blocks * rows
@@ -1000,21 +1174,23 @@
             seq, seq, pl.BlockSpec((rows, 3 * width), lambda s: (at(s), 0)),
             pl.BlockSpec((1, HEADS // 2, 2 * rows, rows), lambda s: (at(s), 0, 0, 0)),
         ] + [whole(v.shape) for v in (vec, sums, wqkv, wo)] + [ANYWHERE] * 12,
-        out_specs=[seq] + [in_vmem] * 7 + [ANYWHERE] * 2,
+        out_specs=[seq] + [in_vmem] * 7 + [ANYWHERE] * 3,
         out_shape=[sds(*x.shape)] + [sds(*s, dtype=F32) for s in shapes]
-        + [sds(SUM_ROWS, width, dtype=F32), sds(*home), sds(tok, 3 * width)],
+        + [sds(SUM_ROWS, width, dtype=F32), sds(*home), sds(tok, 3 * width), sds(tok, width)],
         scratch_shapes=[
             pltpu.VMEM((2, tok, width), BF16), pltpu.VMEM((2, tok, width), BF16), pltpu.VMEM((SLOTS, width, width), BF16),
-            pltpu.VMEM((UNITS, 4, 4 * small, width), BF16), pltpu.VMEM((UNITS, 2, 4 * small, width), BF16),
-            pltpu.VMEM((UNITS, 4 * small, width), BF16), pltpu.VMEM((UNITS, 4, small, width), BF16),
-            pltpu.VMEM((UNITS, 3, small, width), BF16), pltpu.VMEM((2, rows, 3 * width), BF16),
+            pltpu.VMEM((UNITS, 4, 4 * small, width), BF16),
+            pltpu.VMEM((UNITS, 2, 2, 4 * small, width // 2), BF16), pltpu.VMEM((UNITS, 2, 4 * small, width // 2), BF16),
+            pltpu.VMEM((8, 4, small, width), BF16),
+            pltpu.VMEM((UNITS, 5, small, width), BF16), pltpu.VMEM((2, rows, 3 * width), BF16),
+            pltpu.VMEM((2, rows, width), BF16), pltpu.VMEM((rest.shape[0] // 4, 4, *rest.shape[1:]), BF16),
             pltpu.VMEM((SUM_ROWS, 8, width), F32), pltpu.VMEM((5, SUM_ROWS, width), F32), pltpu.VMEM((6, SUM_ROWS, width), F32),
-            dma((2,)), dma((2,)), dma((UNITS, 10)), dma((UNITS, 10)), dma((6,)), dma((6,)), dma((2,)), dma((blocks,)),
-            dma((blocks, 3)), dma((blocks, 3)),
+            dma((2,)), dma((2,)), dma((UNITS, 16)), dma((UNITS, 16)), dma((6,)), dma((6,)), dma((2,)), dma((2,)), dma((blocks,)),
+            dma((blocks, 3)), dma((blocks, 3)), dma(()), dma((3,)), dma((3,)),
         ],
         compiler_params=params(2),
         name="last",
-    )(x, g1, qkv, pt, vec, sums, wqkv, wo, z, g, a3, dh, ot, gt, a2, dp, a1, o, g1.reshape(tok, width), out)
+    )(x, g1, qkv, pt, vec, sums, wqkv, wo, z, g, a3, dh, ot, gt, a2, dp, a1, o, rest, out)
     return result[0], result[1:7], result[7], result[8]
 
 
@@ -1022,10 +1198,10 @@
     clips, frames, places, width = inputs.shape
     x = inputs.reshape(clips * frames, places, width)
     (a1, qkv, pt, o), x1, (wqkv, wo, tqkv, to, win, wout), vec = first(x, vec, shards, clips)
-    out, g1, g, a2, dp, ot, gt, a3, z, dh, sums = middle(x1, cotangent, vec, tqkv, to, win, wout)
+    out, g1, rest, g, a2, dp, ot, gt, a3, z, dh, sums = middle(x1, cotangent, vec, tqkv, to, win, wout)
     saved = (z, g, a3, dh, ot, gt, a2, dp, a1, o, qkv, pt, sums)
     dx, grads, rows, output = last(
-        x, g1.reshape(x.shape), inputs.shape, saved, vec, wqkv, wo, out, [s.shape for s in shards]
+        x, g1.reshape(x.shape), rest, inputs.shape, saved, vec, wqkv, wo, out, [s.shape for s in shards]
     )
     return output, dx.reshape(inputs.shape), grads, rows
 

time: 474 us -> 427 us (0.901)
  Pallas kernels: 455 us -> 409 us
    pallas_call x1, Pallas kernels: 174 us -> 147 us  [last(): pl.pallas_call(last_kernel, grid=(STEPS,), in_specs=[seq, seq, pl.BlockSp...]
    pallas_call x1, Pallas kernels: 133 us -> 121 us  [first(): pl.pallas_call(first_kernel, grid=(blocks,), in_specs=[seq, whole(vec.sha...]
    pallas_call x1, Pallas kernels: 149 us -> 140 us  [middle(): pl.pallas_call(middle_kernel, grid=(blocks,), in_specs=[pl.BlockSpec((1,...]
where the time goes in v2:
time: 427 us
  Pallas kernels  409 us (96%)
  local copies, waits for them, and re-layouts  15.8 us (4%)
    pallas_call x1, Pallas kernels, last(): pl.pallas_call(last_kernel, grid=(STEPS,), in_specs=[seq, seq, pl.BlockSp...  147 us
    pallas_call x1, Pallas kernels, middle(): pl.pallas_call(middle_kernel, grid=(blocks,), in_specs=[pl.BlockSpec((1,...  140 us
    pallas_call x1, Pallas kernels, first(): pl.pallas_call(first_kernel, grid=(blocks,), in_specs=[seq, whole(vec.sha...  121 us
    unnamed x24, local copies, waits for them, and re-layouts  10.5 us

profile of v2, /device:TPU:0, one launch (start us, length us, event | category | flops | bytes accessed | tf_op | source)
XLA Modules:
  0.0 427.0 jit_solution(12196701877411379548)
XLA Ops:
  0.7 1.5 stack.49
  2.1 0.2 dynamic_update_slice.9
  2.3 0.8 dynamic_update_slice.11
  3.2 0.7 maximum_convert_fusion
  3.9 0.2 dynamic_update_slice.10
  4.1 0.6 fusion.4.vec_ref
  4.7 121.5 %first.1 = (bf16[2048,768]{1,0:T(8,128)(2,1)}, bf16[2048,2304]{1,0:T(8,128)(2,1)}, bf16[8,6,512,256]{3,2,1,0:T(8,128)(2,1)}, bf16[2048,768]{1,0:T(8,128)(2,1)}, ...) custom-call(bf16[8,256,768]{2,1,0:T(8,128)(2,1)} %bitcast.46, ...), custom_call_target="tpu_custom_call" | custom-call | tf_op jit(solution)/shard_map/first/pallas_call | solution.py:680
  126.2 140.3 %middle.1 = (bf16[8,16,16,768]{3,2,1,0:T(8,128)(2,1)}, bf16[2,4,256,768]{3,2,1,0:T(8,128)(2,1)}, bf16[16,16,768]{2,1,0:T(8,128)(2,1)}, bf16[2048,768]{1,0:T(8,12...) custom-call(bf16[2,16,64,768]{3,2,1,0:T(8,128)(2,1)} %get-tuple-elem, ...), custom_call_target="tpu_custom_call" | custom-call | tf_op jit(solution)/shard_map/middle/pallas_call | solution.py:786
  266.5 147.4 %last.1 = (bf16[8,256,768]{2,1,0:T(8,128)(2,1)}, f32[24,2304]{1,0:T(8,128)}, f32[24,768]{1,0:T(8,128)}, f32[24,2304]{1,0:T(8,128)}, f32[24,768]{1,0:T(8,128)}, /...) custom-call(bf16[8,256,768]{2,1,0:T(8,128)(2,1)} %bitcast.47, ...), custom_call_target="tpu_custom_call" | custom-call | tf_op jit(solution)/shard_map/last/pallas_call | solution.py:1170
  413.8 0.8 slice.42
  414.6 0.6 dynamic-slice_bitcast_fusion
  415.3 0.8 slice_bitcast_fusion
  416.1 0.1 constant_dynamic-slice_fusion.2
  416.2 0.5 slice_bitcast_fusion.1
  416.7 0.6 fusion.5
  417.3 3.9 copy.52
  421.2 0.0 copy-done
  421.2 0.0 copy-start.5
  421.2 0.0 copy-start.2
  421.3 0.0 copy-start.1
  421.3 1.7 copy.53
  422.9 0.0 copy-done.4
  422.9 0.7 copy.54
  423.6 0.0 copy-done.6
  423.6 0.6 copy.55
  424.3 0.0 copy-done.3
  424.3 0.7 copy.56
  424.9 0.0 copy-done.5
  424.9 0.6 copy.57
  425.6 0.0 copy-done.2
  425.6 0.7 copy.58
  426.3 0.7 copy.59
  (13 shorter events, 0.1 us)
Async XLA Ops:
  417.3 3.9 copy-start
  421.2 1.7 copy-start.4
  421.2 2.4 copy-start.6
  421.2 3.0 copy-start.3
  421.2 3.7 copy-start.5
  421.2 4.3 %copy-start.2 = (f32[24,3072]{1,0:T(8,128)S(1)}, f32[24,3072]{1,0:T(8,128)}, u32[]{:S(2)}) copy-start(f32[24,3072]{1,0:T(8,128)} %get-tuple-element.135) | copy-start | bytes 884740
  421.3 5.0 %copy-start.1 = (f32[96,768]{1,0:T(8,128)S(1)}, f32[96,768]{1,0:T(8,128)}, u32[]{:S(2)}) copy-start(f32[96,768]{1,0:T(8,128)} %get-tuple-element.137) | copy-start | bytes 884740

commit v3 on v2

--- a/solution.py
+++ b/solution.py
@@ -110,7 +110,7 @@
 LONG = 10
 VEC_ROWS = 32
 SUM_ROWS = 24
-VMEM_LIMIT = 61 * 2**20
+VMEM_LIMIT = 62 * 2**20
 
 
 def row(vec_ref, i):
@@ -135,7 +135,7 @@
 
 
 def place_rows(
-    x1, take_g, period, vec_ref, wqkv_ref, wo_ref, win_ref, wout_ref, a2_ref, dp_ref, o_ref, gt_ref, a3_ref, z_ref, dh_ref,
+    x1, take_g, midway, period, vec_ref, wqkv_ref, wo_ref, win_ref, wout_ref, a2_ref, dp_ref, o_ref, gt_ref, a3_ref, z_ref, dh_ref,
     sum_ref, qkv_ref, pt_ref,
 ):
     rows, width = x1.shape
@@ -166,6 +166,8 @@
         dh_ref[:, sl] = dh
         sum_ref[BIN + i] += fold(dh.astype(F32))
         da3 = da3 + dot_nt(dh, win_ref[:, sl])
+        if i == 1:
+            midway()
     sum_ref[GAIN3] += fold(da3 * hat3)
     sum_ref[SHIFT3] += fold(da3)
     dx2 = g + norm_back(da3, hat3, rstd3, row(vec_ref, GAIN3))
@@ -235,7 +237,7 @@
     def take_g():
         return g_ref[0].reshape(rows, width)
 
-    out, dx1 = place_rows(x1, take_g, places, vec_ref, wqkv_ref, wo_ref, win_ref, wout_ref, *rest)
+    out, dx1 = place_rows(x1, take_g, lambda: None, places, vec_ref, wqkv_ref, wo_ref, win_ref, wout_ref, *rest)
     out_ref[0] = out.reshape(frames, places, width)
     dx1_ref[0] = dx1.reshape(frames, places, width)
 
@@ -553,12 +555,14 @@
     def start(self):
         for copy in self.copies():
             copy.start()
-        self.own().start()
+        if self.local is not None:
+            self.own().start()
 
     def arrive(self):
         for copy in self.copies():
             copy.wait_recv()
-        self.own().wait()
+        if self.local is not None:
+            self.own().wait()
 
     def drain(self):
         for copy in self.copies():
@@ -569,66 +573,114 @@
     return pl.ds(pl.multiple_of(start, size), size)
 
 
-GATHERED = ((0, 0), (0, 1), (0, 2), (1, 0), (2, 0), (2, 1), (2, 2), (3, 0), (4, 0), (4, 1), (4, 2), (4, 3), (5, 0))
+GATHERED = ((0, 0), (0, 1), (0, 2), (1, 0), (2, 0), (2, 1), (2, 2), (3, 0), (5, 0), (4, 0), (4, 1), (4, 2), (4, 3))
 BEFORE = {
-    0: ("0 0", "0 1", "0 2", "0 3", "1 0", "1 1", "0 4", "0 5", "2 0", "0 6", "1 2", "0 7", "0 8", "0 9", "2 1", "a 4", "1 3", "a 5", "a 6", "a 7", "3 0", "a 8", "2 2", "a 9", "0 10", "4 0", "0 11", "0 12", "3 1", "b 4", "2 3", "b 5", "b 6", "a 10", "4 1", "b 7", "a 11", "3 2", "b 8", "a 12", "3 3", "1 4", "b 9", "4 2", "4 3"),
-    1: ("2 4", "1 5", "b 10", "b 11", "b 12"),
-    2: ("3 4", "1 6", "2 5"),
-    3: ("4 4", "2 6", "1 7"),
-    4: ("3 5", "3 6", "1 8"),
-    5: ("4 5", "4 6", "2 7", "2 8"),
-    6: ("3 7", "1 9"),
-    7: ("4 7", "3 8", "2 9", "1 10"),
+    0: (0, 1, 2, 3, 300, 301, 4, 5, 400, 6, 302, 7, 8, 401, 303, 104, 105, 500, 106, 402, 107, 9, 600, 108, 501, 403, 204, 109, 10, 601, 205, 206, 11, 502, 207, 503, 304, 110, 12, 602, 208, 603),
+    1: (404, 305, 306, 209, 210, 111, 112),
+    2: (504, 405, 307),
+    3: (604, 406, 308, 211, 212, 505, 407),
+    4: (605, 506),
+    5: (606,),
+    6: (408,),
+    7: (507, 309),
 }
-AFTER = ("1 11", "1 12", "4 8", "3 9", "2 10", "2 11", "4 9", "2 12", "3 10", "3 11", "4 10", "4 11", "3 12", "4 12")
-VEC_AT = ("1 0", "1 2", "2 1", "3 1")
-
-
-def first_kernel(x_ref, vec_ref, *refs):
+EARLY = (310, 311, 312, 607)
+LATE = (508, 409, 410, 608, 411, 412, 509, 510, 609, 511, 610, 512, 611, 612)
+VEC_AT = (300, 302, 401, 501)
+AFTER_SPACE = {0: (0,), 1: (1,), 2: (2,), 3: (3,), 7: (100,)}
+AT_PLACE = {
+    (0, 0): (101,), (0, 1): (4,), (0, 2): (102,), (1, 0): (5,), (1, 2): (103,),
+    (2, 0): (6,), (2, 2): (7,), (3, 0): (104,), (3, 2): (105,), (4, 0): (106,),
+    (4, 2): (107,), (5, 2): (200,), (6, 0): (201,), (6, 2): (202,), (7, 0): (203,), (7, 2): (204,),
+}
+KEPT = 5
+
+
+def front_kernel(x_ref, vec_ref, cot_ref, *refs):
     shards = refs[:6]
-    a_ref, qkv_ref, pt_ref, o_ref, land_ref = refs[6:11]
-    fulls, vec_out = refs[11:17], refs[17]
-    wqkv_ref, wo_ref, x1_ref = refs[18:21]
+    a_ref, qkv_ref, pt_ref, o_ref = refs[6:10]
+    land_ref, home_ref, wqkv_out, wo_out, vec_out = refs[10:15]
+    out_all, out_home, rest_all, g_ref = refs[15:19]
+    kept_refs = refs[19:27]
+    sum_ref = kept_refs[7]
+    weights = refs[27:33]
+    x1_ref, tqkv_ref, tpt_ref, gland, dx1_ref, xin, out_ref = refs[33:40]
     count = len(GATHERED)
-    zbufs, groups = refs[21 : 21 + count], refs[21 + count : 21 + 2 * count]
-    held, got, local, send, recv, vsend, vrecv, keep, xlocal, xsend, xrecv = refs[21 + 2 * count :]
+    refs = refs[40:]
+    zbufs, groups = refs[:count], refs[count : 2 * count]
+    held, got, local, send, recv, vsend, vrecv, keep, xlocal, xsend, xrecv = refs[2 * count : 2 * count + 11]
+    glocal, gsend, grecv, dlocal, dsend, drecv, xload, gkeep, okeep, dkeep = refs[2 * count + 11 :]
     step = pl.program_id(0)
     blocks, rows, width = x1_ref.shape
-    per = land_ref.shape[1] // 4
-    part = rows // 4
+    _, frames, part, _ = gland.shape
+    clips, per, places, _ = cot_ref.shape
+    chunks, mine = blocks // clips, places // 4
     z = lax.axis_index("seq")
     peers = partners()
     vec = Sum(peers, held, got, vsend, vrecv)
-    homes = (wqkv_ref, wo_ref) + tuple(fulls[2:])
 
     def piece(u):
         w, at = GATHERED[u]
-        return (ref.at[:, pl.ds(at * width, width)] for ref in (shards[w], homes[w]))
+        return (ref.at[:, pl.ds(at * width, width)] for ref in (shards[w], weights[w]))
 
     work = []
     for u in range(count):
         shard, full = piece(u)
         work.append(Gather(peers, u < 4, shard, zbufs[u], groups[u], full, local.at[u], send.at[u], recv.at[u]))
 
-    def swap(b):
+    def swap_x1(b):
         return Swap(
-            peers, lambda to: x1_ref.at[b, rows_at(to * part, part)], land_ref.at[b // per, z * per + lax.rem(b, per)],
+            peers, lambda to: x1_ref.at[b, rows_at(to * mine, mine)], land_ref.at[b // per, z * per + lax.rem(b, per)],
             xlocal.at[b], xsend.at[b], xrecv.at[b],
         )
 
+    def swap_cot(b):
+        return Swap(
+            peers, lambda to: cot_ref.at[b // chunks, :, rows_at(to * mine + (b % chunks) * part, part)],
+            gland.at[b, pl.ds(z * per, per)], glocal.at[b], gsend.at[b], grecv.at[b],
+        )
+
+    def swap_dx1(b):
+        return Swap(
+            peers, lambda to: dx1_ref.at[b, pl.ds(to * per, per)],
+            home_ref.at[b // chunks, :, rows_at(z * mine + (b % chunks) * part, part)], dlocal.at[b], dsend.at[b], drecv.at[b],
+        )
+
+    def out_copies(b):
+        own = out_home.at[b // chunks, :, rows_at(z * mine + (b % chunks) * part, part)]
+        return (
+            pltpu.make_async_copy(out_ref.at[b % 2], out_all.at[b], okeep.at[b % 2, 0]),
+            pltpu.make_async_copy(out_ref.at[b % 2, pl.ds(z * per, per)], own, okeep.at[b % 2, 1]),
+        )
+
+    def dx1_copies(b):
+        own = home_ref.at[b // chunks, :, rows_at(z * mine + (b % chunks) * part, part)]
+        return (
+            pltpu.make_async_copy(dx1_ref.at[KEPT + b % 2], rest_all.at[b - KEPT], dkeep.at[b % 2, 0]),
+            pltpu.make_async_copy(dx1_ref.at[KEPT + b % 2, pl.ds(z * per, per)], own, dkeep.at[b % 2, 1]),
+        )
+
+    def load_x1(b):
+        src = land_ref.at[b // chunks, :, rows_at((b % chunks) * part, part)]
+        return pltpu.make_async_copy(src, xin.at[b % 2], xload.at[b % 2])
+
+    def g_out(b):
+        return pltpu.make_async_copy(gland.at[b], g_ref.at[b], gkeep.at[b])
+
     def kept(i):
-        return pltpu.make_async_copy(homes[i], fulls[i], keep.at[i])
-
-    def event(name):
-        stage, i = name.split()
-        getattr(work[int(i)], "step" + stage)()
+        return pltpu.make_async_copy(weights[i], (wqkv_out, wo_out)[i], keep.at[i])
+
+    def event(code):
+        w = work[code % 100]
+        (w.step0, w.stepa, w.stepb, w.step1, w.step2, w.step3, w.step4)[code // 100]()
 
     @pl.when(step == 0)
     def _():
+        sum_ref[...] = jnp.zeros_like(sum_ref)
         held[0] = vec_ref[...]
         enter(peers)
         vec.start(0)
-        for k, name in enumerate(BEFORE[0]):
+        for name in BEFORE[0]:
             event(name)
             if name in VEC_AT:
                 level = VEC_AT.index(name)
@@ -646,15 +698,95 @@
             for name in BEFORE[k]:
                 event(name)
 
-    x1_ref[step] = space_rows(
-        x_ref[0].astype(F32), vec_out, wqkv_ref, wo_ref, a_ref, qkv_ref, pt_ref.at[0], o_ref
-    )
-    swap(step).start()
-
-    @pl.when(step == blocks - 1)
+    def exchange(code):
+        (swap_x1, swap_cot, swap_dx1)[code // 100](code % 100).start()
+
+    def at(point):
+        for (b, where), names in AT_PLACE.items():
+            if where == point:
+
+                @pl.when(step == blocks + b)
+                def _(names=names):
+                    for name in names:
+                        exchange(name)
+
+    @pl.when(step < blocks)
     def _():
-        for name in AFTER:
-            event(name)
+        x1_ref[step] = space_rows(
+            x_ref[0].astype(F32), vec_out, weights[0], weights[1], a_ref, qkv_ref, pt_ref.at[0], o_ref
+        )
+
+        for k, names in AFTER_SPACE.items():
+
+            @pl.when(step == k)
+            def _(names=names):
+                for name in names:
+                    exchange(name)
+
+    @pl.when(step >= blocks)
+    def _():
+        b = step - blocks
+        slot = lax.rem(b, 2)
+        at(0)
+
+        @pl.when(b == 0)
+        def _():
+            for name in EARLY:
+                event(name)
+
+        @pl.when(lax.rem(b, chunks) == 0)
+        def _():
+            def arrived(k, _):
+                swap_x1((b // chunks) * per + k).arrive()
+                return 0
+
+            lax.fori_loop(0, per, arrived, 0)
+            load_x1(b).start()
+
+        load_x1(b).wait()
+
+        @pl.when(lax.rem(b, chunks) < chunks - 1)
+        def _():
+            load_x1(b + 1).start()
+
+        def take_g():
+            at(1)
+
+            @pl.when(b == 0)
+            def _():
+                for name in LATE:
+                    event(name)
+
+            swap_cot(b).arrive()
+            g_out(b).start()
+            return gland[b].reshape(rows, width)
+
+        x1 = xin[slot].reshape(rows, width).astype(F32)
+        out, dx1 = place_rows(x1, take_g, lambda: at(2), part, vec_out, *weights[2:], *kept_refs, tqkv_ref, tpt_ref)
+
+        @pl.when(b >= 2)
+        def _():
+            for copy in out_copies(b - 2):
+                copy.wait()
+
+        out_ref[slot] = out.reshape(frames, part, width)
+        for copy in out_copies(b):
+            copy.start()
+
+        @pl.when(b >= KEPT + 2)
+        def _():
+            for copy in dx1_copies(b - 2):
+                copy.wait()
+
+        dx1_ref[jnp.where(b < KEPT, b, KEPT + slot)] = dx1.reshape(frames, part, width)
+
+        @pl.when(b >= KEPT)
+        def _():
+            for copy in dx1_copies(b):
+                copy.start()
+
+    @pl.when(step == 2 * blocks - 1)
+    def _():
         kept(0).wait()
         kept(1).wait()
         vec.drain()
@@ -662,149 +794,83 @@
             w.drain()
 
         def finish(b, _):
-            swap(b).arrive()
-            swap(b).drain()
+            swap_x1(b).drain()
+            swap_cot(b).drain()
+            g_out(b).wait()
             return 0
 
         lax.fori_loop(0, blocks, finish, 0)
 
-
-def first(x, vec, shards, clips):
+        for b in (blocks - 2, blocks - 1):
+            for copy in out_copies(b) + dx1_copies(b):
+                copy.wait()
+
+        def finish_dx1(b, _):
+            swap_dx1(b).arrive()
+            swap_dx1(b).drain()
+            return 0
+
+        lax.fori_loop(0, KEPT, finish_dx1, 0)
+
+
+def front(x, cot, vec, shards):
     blocks, rows, width = x.shape
+    clips, per, places, _ = cot.shape
+    frames = 4 * per
+    part = rows // frames
     tok = blocks * rows
-    frames = blocks // clips
     count = len(GATHERED)
     dma = pltpu.SemaphoreType.DMA
-    seq = pl.BlockSpec((1, rows, width), lambda b: (b, 0, 0))
-    fixed = pl.BlockSpec((VEC_ROWS, width), lambda b: (0, 0))
+
+    def one(s):
+        return jnp.minimum(s, blocks - 1)
+
+    def two(s):
+        return jnp.maximum(s - blocks, 0)
+
+    def early(*shape):
+        return pl.BlockSpec(shape, lambda s: (one(s),) + (0,) * (len(shape) - 1))
+
+    def late(*shape):
+        return pl.BlockSpec(shape, lambda s: (two(s),) + (0,) * (len(shape) - 1))
+
+    fixed = pl.BlockSpec((VEC_ROWS, width), lambda s: (0, 0))
+    full = [(32 * s.shape[0], s.shape[1]) for s in shards]
+    ff = full[4][1]
+    place = (blocks, frames, part, width)
+    token_widths = (width, 3 * width, width, width, width, ff, ff)
     out = pl.pallas_call(
-        first_kernel,
-        grid=(blocks,),
-        in_specs=[seq, whole(vec.shape)] + [ANYWHERE] * 6,
-        out_specs=[rows_spec(rows, width), rows_spec(rows, 3 * width), probs_spec(rows), rows_spec(rows, width), ANYWHERE]
-        + [ANYWHERE] * 6 + [fixed],
+        front_kernel,
+        grid=(2 * blocks,),
+        in_specs=[early(1, rows, width), whole(vec.shape)] + [ANYWHERE] * 7,
+        out_specs=[
+            early(rows, width), early(rows, 3 * width), early(1, HEADS // 2, 2 * rows, rows), early(rows, width),
+            ANYWHERE, ANYWHERE, ANYWHERE, ANYWHERE, fixed, ANYWHERE, ANYWHERE, ANYWHERE, ANYWHERE,
+        ] + [late(rows, w) for w in token_widths] + [pl.BlockSpec((SUM_ROWS, 8, width), lambda s: (0, 0, 0))],
         out_shape=[
             sds(tok, width), sds(tok, 3 * width), sds(blocks, HEADS // 2, 2 * rows, rows), sds(tok, width),
-            sds(clips, 4 * frames, rows // 4, width),
-        ] + [sds(32 * s.shape[0], s.shape[1]) for s in shards] + [sds(VEC_ROWS, width, dtype=F32)],
-        scratch_shapes=[
-            pltpu.VMEM((width, 3 * width), BF16), pltpu.VMEM((width, width), BF16), pltpu.VMEM((blocks, rows, width), BF16)
+            sds(clips, frames, places // 4, width), sds(*cot.shape), sds(*full[0]), sds(*full[1]),
+            sds(VEC_ROWS, width, dtype=F32), sds(*place), sds(*cot.shape), sds(blocks - KEPT, *place[1:]),
+            sds(*place),
+        ] + [sds(tok, w) for w in token_widths] + [sds(SUM_ROWS, 8, width, dtype=F32)],
+        scratch_shapes=[pltpu.VMEM(s, BF16) for s in full]
+        + [
+            pltpu.VMEM((blocks, rows, width), BF16), pltpu.VMEM((rows, 3 * width), BF16),
+            pltpu.VMEM((HEADS // 2, 2 * rows, rows), BF16), pltpu.VMEM(place, BF16),
+            pltpu.VMEM((KEPT + 2, *place[1:]), BF16), pltpu.VMEM((2, *place[1:]), BF16), pltpu.VMEM((2, *place[1:]), BF16),
         ]
         + [pltpu.VMEM((4, shards[w].shape[0], width), BF16) for w, _ in GATHERED]
         + [pltpu.VMEM((4 * shards[w].shape[0], width), BF16) for w, _ in GATHERED]
         + [
             pltpu.VMEM((5, *vec.shape), BF16), pltpu.VMEM((6, *vec.shape), BF16), dma((count, 2)), dma((count, 18)),
-            dma((count, 18)),
-            dma((6,)), dma((6,)), dma((2,)), dma((blocks,)), dma((blocks, 3)), dma((blocks, 3)),
+            dma((count, 18)), dma((6,)), dma((6,)), dma((2,)), dma((blocks,)), dma((blocks, 3)), dma((blocks, 3)),
+            dma((blocks,)), dma((blocks, 3)), dma((blocks, 3)), dma((KEPT,)), dma((KEPT, 3)), dma((KEPT, 3)), dma((2,)), dma((blocks,)),
+            dma((2, 2)), dma((2, 2)),
         ],
         compiler_params=params(0),
-        name="first",
-    )(x, vec.astype(BF16), *shards)
-    return out[:4], out[4], out[5:11], out[11]
-
-
-def middle_kernel(x1_ref, cot_ref, vec_ref, wqkv_ref, wo_ref, win_ref, wout_ref, *refs):
-    out_ref, home_ref, rest_ref, g_ref = refs[:4]
-    rest = refs[4:12]
-    sum_ref = rest[7]
-    qkv_ref, pt_ref, gland, dx1_ref, glocal, gsend, grecv, xlocal, xsend, xrecv = refs[12:]
-    step = pl.program_id(0)
-    blocks, frames, part, width = gland.shape
-    rows = frames * part
-    clips, per, places, _ = cot_ref.shape
-    chunks = blocks // clips
-    mine = places // 4
-    z = lax.axis_index("seq")
-    peers = partners()
-
-    def swap_in(b):
-        clip, chunk = b // chunks, b % chunks
-        return Swap(
-            peers, lambda to: cot_ref.at[clip, :, rows_at(to * mine + chunk * part, part)],
-            gland.at[b, pl.ds(z * per, per)], glocal.at[b], gsend.at[b], grecv.at[b],
-        )
-
-    def swap_out(b):
-        clip, chunk = b // chunks, b % chunks
-        return Swap(
-            peers, lambda to: dx1_ref.at[b, pl.ds(to * per, per)],
-            home_ref.at[clip, :, rows_at(z * mine + chunk * part, part)], xlocal.at[b], xsend.at[b], xrecv.at[b],
-        )
-
-    @pl.when(step == 0)
-    def _():
-        sum_ref[...] = jnp.zeros_like(sum_ref)
-        enter({k: v for k, v in peers.items() if k[0] == "z"})
-
-        def begin(b, _):
-            swap_in(b).start()
-            return 0
-
-        lax.fori_loop(0, blocks, begin, 0)
-
-    def take_g():
-        swap_in(step).arrive()
-        g16 = gland[step].reshape(rows, width)
-        g_ref[...] = g16
-        return g16
-
-    x1 = x1_ref[0].reshape(rows, width).astype(F32)
-    out, dx1 = place_rows(x1, take_g, part, vec_ref, wqkv_ref, wo_ref, win_ref, wout_ref, *rest, qkv_ref, pt_ref)
-    out_ref[0] = out.reshape(frames, part, width)
-    dx1_ref[step] = dx1.reshape(frames, part, width)
-
-    @pl.when(step < blocks - 1)
-    def _():
-        swap_out(step).start()
-
-    @pl.when(step == blocks - 1)
-    def _():
-        rest_out = pltpu.make_async_copy(dx1_ref.at[blocks - 1], rest_ref, xlocal.at[blocks - 1])
-        rest_out.start()
-
-        def finish(b, _):
-            swap_in(b).drain()
-            swap_out(b).arrive()
-            swap_out(b).drain()
-            return 0
-
-        lax.fori_loop(0, blocks - 1, finish, 0)
-        swap_in(blocks - 1).drain()
-        rest_out.wait()
-
-
-def middle(x1, cot, vec, wqkv, wo, win, wout):
-    clips, frames, mine, width = x1.shape
-    rows = 256
-    part = rows // frames
-    per = mine // part
-    blocks = clips * per
-    tok = blocks * rows
-    ff = win.shape[1]
-    dma = pltpu.SemaphoreType.DMA
-    n = rows_spec(rows, width)
-    return pl.pallas_call(
-        middle_kernel,
-        grid=(blocks,),
-        in_specs=[pl.BlockSpec((1, frames, part, width), lambda b: (b // per, 0, b % per, 0)), ANYWHERE]
-        + [whole(w.shape) for w in (vec, wqkv, wo, win, wout)],
-        out_specs=[
-            pl.BlockSpec((1, frames, part, width), lambda b: (b, 0, 0, 0)), ANYWHERE, ANYWHERE, n, n,
-            rows_spec(rows, 3 * width), n, n, n, rows_spec(rows, ff), rows_spec(rows, ff), pl.BlockSpec((SUM_ROWS, 8, width), lambda b: (0, 0, 0)),
-        ],
-        out_shape=[
-            sds(blocks, frames, part, width), sds(*cot.shape), sds(frames, part, width), sds(tok, width), sds(tok, width), sds(tok, 3 * width),
-            sds(tok, width), sds(tok, width), sds(tok, width), sds(tok, ff), sds(tok, ff),
-            sds(SUM_ROWS, 8, width, dtype=F32),
-        ],
-        scratch_shapes=[
-            pltpu.VMEM((rows, 3 * width), BF16), pltpu.VMEM((HEADS // 2, 2 * rows, rows), BF16),
-            pltpu.VMEM((blocks, frames, part, width), BF16), pltpu.VMEM((blocks, frames, part, width), BF16),
-            dma((blocks,)), dma((blocks, 3)), dma((blocks, 3)), dma((blocks,)), dma((blocks, 3)), dma((blocks, 3)),
-        ],
-        compiler_params=params(1),
-        name="middle",
-    )(x1, cot, vec, wqkv, wo, win, wout)
+        name="front",
+    )(x, vec.astype(BF16), cot, *shards)
+    return out[:4], out[5], out[6:8], out[8], out[9:12], out[12:]
 
 
 class Scatter:
@@ -945,37 +1011,37 @@
 CHAINED = 12
 STEPS = PANELS + BLOCKS + UNITS - PANELS
 AFTER_STEP = {
-    3: ("0 0", "0 1", "0 2", "0 3"),
-    4: ("0 4",),
-    5: ("0 5", "1 0", "1 1"),
-    6: ("0 6", "1 2"),
-    7: ("0 7", "1 3", "1 4", "2 0"),
-    8: ("0 8", "2 1"),
-    9: ("0 9", "2 2", "1 5"),
-    10: ("0 10", "2 3", "2 4"),
-    11: ("1 6", "1 7", "3 0", "3 1", "3 2"),
-    12: ("2 5", "1 8", "1 9", "3 3", "3 4", "2 6", "b 0"),
-    13: ("2 7", "1 10", "b 1", "b 2", "3 5"),
-    14: ("2 8", "2 9", "c 0", "3 6"),
-    15: ("2 10", "b 3", "b 4", "c 1", "3 7"),
-    16: ("c 2",),
-    17: ("b 5",),
-    18: ("b 6", "4 0", "3 8"),
-    19: ("0 11", "c 3", "c 4"),
-    20: ("0 12", "b 7", "c 5", "c 6", "4 1", "1 11", "3 9"),
-    21: ("0 13", "1 12", "b 8", "c 7", "4 2", "3 10"),
-    22: ("0 14", "2 11", "1 13", "b 9", "c 8", "4 3", "4 4", "4 5", "4 6", "2 12", "b 10"),
-    23: ("0 15", "1 14", "c 9", "3 11", "4 7", "c 10"),
+    3: (0, 1, 2, 3),
+    4: (4,),
+    5: (5, 100),
+    6: (6, 101),
+    7: (7, 102),
+    8: (8, 103, 200, 201),
+    9: (9, 104, 202),
+    10: (10, 203),
+    11: (105, 300, 301, 204),
+    12: (106, 302, 303, 107),
+    13: (205, 108, 304),
+    14: (206, 207, 109, 305),
+    15: (208, 110, 306),
+    16: (209, 400, 401, 307),
+    17: (210, 402, 403),
+    18: (404,),
+    19: (11, 405),
+    20: (12,),
+    21: (13, 111, 406),
+    22: (14, 112, 500, 501, 407, 113, 506),
+    23: (15, 211, 502, 503, 600, 601, 606, 114, 507, 308, 309, 212),
 }
-TAIL = ("4 8", "2 13", "3 12", "1 15", "4 9", "b 11", "2 14", "4 10", "3 13", "4 12", "c 11", "2 15", "3 14", "4 11", "4 13", "3 15", "4 14", "4 15")
-OUT_AT = (0, 3, 6, 9, 12, 13, 14, 15)
+TAIL = (602, 310, 603, 504, 505, 607, 408, 409, 115, 213, 311, 604, 605, 508, 214, 509, 410, 312, 608, 609, 411, 215, 510, 313, 314, 511, 612, 315, 610, 611, 613, 614, 615)
+OUT_AT = (6, 9, 11, 13, 15, 17, 19, 21)
 
 
 def last_kernel(
-    x_ref, g1_ref, qkv_ref, pt_ref, vec_ref, sums_ref, wqkv_ref, wo_ref, z_ref, g_ref, a3_ref, dh_ref, ot_ref, gt_ref, a2_ref,
-    dp_ref, a1_ref, o_ref, rest_ref, out_ref, dx_ref, sqkv_out, so_out, tqkv_out, to_out, win_out, wout_out, vec_out, home_ref,
-    dps_ref, g1_all, lbuf, rbuf, pieces, core, one, two, zsend, zgot, dpbuf, gbuf, gland, ssum, held, got, lsem, rsem, send, recv, vsend, vrecv,
-    dpsem, gsem, olocal, osend, orecv, rlocal, rsend, rrecv,
+    x_ref, qkv_ref, pt_ref, vec_ref, sums_ref, wqkv_ref, wo_ref, z_ref, g_ref, a3_ref, dh_ref, ot_ref, gt_ref, a2_ref,
+    dp_ref, a1_ref, o_ref, rest_ref, out_ref, g1_in_place, out_in_place, dx_ref, sqkv_out, so_out, tqkv_out, to_out, win_out, wout_out, vec_out, home_ref,
+    dps_ref, g1_home, lbuf, rbuf, pieces, core, one, two, zsend, zgot, dpbuf, gbuf, ssum, held, got, lsem, rsem, send, recv, vsend, vrecv,
+    dpsem, gsem, osend, orecv, rsend, rrecv,
 ):
     step = pl.program_id(0)
     z = lax.axis_index("seq")
@@ -1009,19 +1075,22 @@
         for u in range(UNITS)
     ]
 
-    def event(name):
-        stage, u = name.split()
-        getattr(work[int(u)], "step" + stage)()
+    def event(code):
+        w = work[code % 100]
+        (w.step0, w.step1, w.step2, w.step3, w.stepb, w.stepc, w.step4)[code // 100]()
 
     def swap(b):
         return Swap(
             peers, lambda to: out_ref.at[b, pl.ds(to * per, per)],
-            home_ref.at[b // chunks, :, rows_at(z * mine + (b % chunks) * part, part)], olocal.at[b], osend.at[b], orecv.at[b],
+            home_ref.at[b // chunks, :, rows_at(z * mine + (b % chunks) * part, part)], None, osend.at[b], orecv.at[b],
         )
 
-    rest = Swap(
-        peers, lambda to: rest_ref.at[pl.ds(to * per, per)], gland.at[:, z], rlocal, rsend, rrecv,
-    )
+    def rest(b):
+        return Swap(
+            peers, lambda to: rest_ref.at[b - KEPT, pl.ds(to * per, per)],
+            g1_home.at[b // chunks, :, rows_at(z * mine + (b % chunks) * part, part)], None, rsend.at[b - KEPT],
+            rrecv.at[b - KEPT],
+        )
 
     def load(ref, at, buf, sem, slot):
         src = ref if at is None else ref.at[:, columns(at)]
@@ -1030,12 +1099,18 @@
     def fetch(p, left, l_at, right, r_at):
         slot = lax.rem(p, 2)
         load(left, l_at, lbuf, lsem, slot).start()
-        load(right, r_at, rbuf, rsem, slot).start()
+        if right is g1_home:
+            n = x_ref.shape[1]
+            for b in range(clips * per):
+                src = g1_home.at[b // per, b % per]
+                pltpu.make_async_copy(src, rbuf.at[slot, pl.ds(b * n, n)], rsem.at[slot]).start()
+        else:
+            load(right, r_at, rbuf, rsem, slot).start()
 
     def fetch_panel(p):
         for least, most, left, right, which in (
             (0, 4, z_ref, g_ref, "l"), (4, 8, a3_ref, dh_ref, "r"), (8, 9, ot_ref, gt_ref, ""), (9, 12, a2_ref, dp_ref, "r"),
-            (12, 13, o_ref, g1_all, ""), (13, 16, a1_ref, dps_ref, "r"),
+            (12, 13, o_ref, g1_home, ""), (13, 16, a1_ref, dps_ref, "r"),
         ):
 
             @pl.when((p >= least) & (p < most))
@@ -1046,8 +1121,8 @@
     def dp_out(b):
         return pltpu.make_async_copy(dpbuf.at[b % 2], dps_ref.at[rows_at(b * x_ref.shape[1], x_ref.shape[1])], dpsem.at[b % 2])
 
-    def g1_out(b):
-        return pltpu.make_async_copy(gbuf.at[b % 2], g1_all.at[rows_at(b * x_ref.shape[1], x_ref.shape[1])], gsem.at[b % 2])
+    def g1_in(b):
+        return pltpu.make_async_copy(g1_home.at[b // per, b % per], gbuf.at[b % 2], gsem.at[b % 2])
 
     is_block = (step >= PANELS) & (step < PANELS + BLOCKS)
     panel = jnp.where(step < PANELS, step, step - BLOCKS)
@@ -1057,7 +1132,8 @@
         ssum[...] = sums_ref[...]
         fetch_panel(step)
         enter(peers)
-        rest.start()
+        for b in range(KEPT, blocks):
+            rest(b).start()
 
     for b, at in enumerate(OUT_AT):
 
@@ -1095,21 +1171,24 @@
         @pl.when(b >= 2)
         def _():
             dp_out(b - 2).wait()
-            g1_out(b - 2).wait()
 
         slot = lax.rem(b, 2)
-        gbuf[slot] = g1_ref[0]
-
-        @pl.when(b == BLOCKS - per)
-        def _():
-            rest.arrive()
-
-        @pl.when(b >= BLOCKS - per)
-        def _():
-            for k in range(4):
-                gbuf[slot, pl.ds(k * mine + mine - part, part)] = gland[b - (BLOCKS - per), k]
-
-        g1_out(b).start()
+
+        @pl.when(b == 0)
+        def _():
+            g1_in(b).start()
+
+        @pl.when(b == per - 1)
+        def _():
+            for k in range(KEPT, blocks):
+                rest(k).arrive()
+
+        g1_in(b).wait()
+
+        @pl.when(b < BLOCKS - 1)
+        def _():
+            g1_in(b + 1).start()
+
         dx_ref[0] = space_back_rows(
             x_ref[0].astype(F32), gbuf[slot], qkv_ref, pt_ref.at[0], vec_ref, wqkv_ref, wo_ref, dpbuf.at[lax.rem(b, 2)], ssum
         )
@@ -1119,8 +1198,6 @@
     def _():
         dp_out(step - PANELS - 1).wait()
         dp_out(step - PANELS).wait()
-        g1_out(step - PANELS - 1).wait()
-        g1_out(step - PANELS).wait()
         held[0] = jnp.concatenate([jnp.sum(ssum[i], axis=0, keepdims=True) for i in range(SUM_ROWS)], axis=0)
         vec.start(0)
 
@@ -1143,7 +1220,8 @@
             event(name)
         vec_out[...] = held[4]
         vec.drain()
-        rest.drain()
+        for b in range(KEPT, blocks):
+            rest(b).drain()
         for w in work:
             w.drain()
 
@@ -1155,8 +1233,9 @@
         lax.fori_loop(0, blocks, finish, 0)
 
 
-def last(x, g1, rest, home, saved, vec, wqkv, wo, out, shapes):
+def last(x, home, outs, saved, vec, wqkv, wo, shapes):
     z, g, a3, dh, ot, gt, a2, dp, a1, o, qkv, pt, sums = saved
+    out, out_home, rest = outs
     blocks, rows, width = x.shape
     tok = blocks * rows
     dma = pltpu.SemaphoreType.DMA
@@ -1171,38 +1250,36 @@
         last_kernel,
         grid=(STEPS,),
         in_specs=[
-            seq, seq, pl.BlockSpec((rows, 3 * width), lambda s: (at(s), 0)),
+            seq, pl.BlockSpec((rows, 3 * width), lambda s: (at(s), 0)),
             pl.BlockSpec((1, HEADS // 2, 2 * rows, rows), lambda s: (at(s), 0, 0, 0)),
-        ] + [whole(v.shape) for v in (vec, sums, wqkv, wo)] + [ANYWHERE] * 12,
+        ] + [whole(v.shape) for v in (vec, sums, wqkv, wo)] + [ANYWHERE] * 14,
         out_specs=[seq] + [in_vmem] * 7 + [ANYWHERE] * 3,
         out_shape=[sds(*x.shape)] + [sds(*s, dtype=F32) for s in shapes]
-        + [sds(SUM_ROWS, width, dtype=F32), sds(*home), sds(tok, 3 * width), sds(tok, width)],
+        + [sds(SUM_ROWS, width, dtype=F32), sds(*home.shape), sds(tok, 3 * width), sds(*home.shape)],
         scratch_shapes=[
             pltpu.VMEM((2, tok, width), BF16), pltpu.VMEM((2, tok, width), BF16), pltpu.VMEM((SLOTS, width, width), BF16),
             pltpu.VMEM((UNITS, 4, 4 * small, width), BF16),
             pltpu.VMEM((UNITS, 2, 2, 4 * small, width // 2), BF16), pltpu.VMEM((UNITS, 2, 4 * small, width // 2), BF16),
             pltpu.VMEM((8, 4, small, width), BF16),
             pltpu.VMEM((UNITS, 5, small, width), BF16), pltpu.VMEM((2, rows, 3 * width), BF16),
-            pltpu.VMEM((2, rows, width), BF16), pltpu.VMEM((rest.shape[0] // 4, 4, *rest.shape[1:]), BF16),
+            pltpu.VMEM((2, rows, width), BF16),
             pltpu.VMEM((SUM_ROWS, 8, width), F32), pltpu.VMEM((5, SUM_ROWS, width), F32), pltpu.VMEM((6, SUM_ROWS, width), F32),
-            dma((2,)), dma((2,)), dma((UNITS, 16)), dma((UNITS, 16)), dma((6,)), dma((6,)), dma((2,)), dma((2,)), dma((blocks,)),
-            dma((blocks, 3)), dma((blocks, 3)), dma(()), dma((3,)), dma((3,)),
+            dma((2,)), dma((2,)), dma((UNITS, 16)), dma((UNITS, 16)), dma((6,)), dma((6,)), dma((2,)), dma((2,)),
+            dma((blocks, 3)), dma((blocks, 3)), dma((blocks - KEPT, 3)), dma((blocks - KEPT, 3)),
         ],
+        input_output_aliases={19: 10, 20: 8},
         compiler_params=params(2),
         name="last",
-    )(x, g1, qkv, pt, vec, sums, wqkv, wo, z, g, a3, dh, ot, gt, a2, dp, a1, o, rest, out)
+    )(x, qkv, pt, vec, sums, wqkv, wo, z, g, a3, dh, ot, gt, a2, dp, a1, o, rest, out, home, out_home)
     return result[0], result[1:7], result[7], result[8]
 
 
 def ring_layer(inputs, cotangent, shards, vec):
     clips, frames, places, width = inputs.shape
     x = inputs.reshape(clips * frames, places, width)
-    (a1, qkv, pt, o), x1, (wqkv, wo, tqkv, to, win, wout), vec = first(x, vec, shards, clips)
-    out, g1, rest, g, a2, dp, ot, gt, a3, z, dh, sums = middle(x1, cotangent, vec, tqkv, to, win, wout)
-    saved = (z, g, a3, dh, ot, gt, a2, dp, a1, o, qkv, pt, sums)
-    dx, grads, rows, output = last(
-        x, g1.reshape(x.shape), rest, inputs.shape, saved, vec, wqkv, wo, out, [s.shape for s in shards]
-    )
+    (a1, qkv, pt, o), home, (wqkv, wo), vec, outs, (g, a2, dp, ot, gt, a3, z, dh, sums) = front(x, cotangent, vec, shards)
+    saved = (z, g.reshape(a2.shape), a3, dh, ot, gt, a2, dp, a1, o, qkv, pt, sums)
+    dx, grads, rows, output = last(x, home, outs, saved, vec, wqkv, wo, [s.shape for s in shards])
     return output, dx.reshape(inputs.shape), grads, rows
 
 

time: 427 us -> 419 us (0.981)
  Pallas kernels: 409 us -> 401 us
    pallas_call x3 -> x2, Pallas kernels: 409 us -> 401 us  [the longest x1 242 us: front(): pl.pallas_call(front_kernel, grid=(2 * blocks,), in_specs=[early(1, rows,...]
where the time goes in v3:
time: 419 us
  Pallas kernels  401 us (96%)
  local copies, waits for them, and re-layouts  15.8 us (4%)
    pallas_call x1, Pallas kernels, front(): pl.pallas_call(front_kernel, grid=(2 * blocks,), in_specs=[early(1, rows,...  242 us
    pallas_call x1, Pallas kernels, last(): pl.pallas_call(last_kernel, grid=(STEPS,), in_specs=[seq, pl.BlockSpec((r...  159 us
    unnamed x24, local copies, waits for them, and re-layouts  10.5 us

profile of v3, /device:TPU:0, one launch (start us, length us, event | category | flops | bytes accessed | tf_op | source)
XLA Modules:
  0.0 419.0 jit_solution(16849560589604905115)
XLA Ops:
  0.7 1.5 stack.49
  2.1 0.2 dynamic_update_slice.9
  2.3 0.8 dynamic_update_slice.11
  3.2 0.7 maximum_convert_fusion
  3.9 0.2 dynamic_update_slice.10
  4.1 0.6 fusion.4.vec_ref
  4.7 241.8 %front.1 = (bf16[2048,768]{1,0:T(8,128)(2,1)}, bf16[2048,2304]{1,0:T(8,128)(2,1)}, bf16[8,6,512,256]{3,2,1,0:T(8,128)(2,1)}, bf16[2048,768]{1,0:T(8,128)(2,1)}, ...) custom-call(bf16[8,256,768]{2,1,0:T(8,128)(2,1)} %bitcast.46, ...), custom_call_target="tpu_custom_call" | custom-call | tf_op jit(solution)/shard_map/front/pallas_call | solution.py:842
  246.5 159.2 %last.1 = (bf16[8,256,768]{2,1,0:T(8,128)(2,1)}, f32[24,2304]{1,0:T(8,128)}, f32[24,768]{1,0:T(8,128)}, f32[24,2304]{1,0:T(8,128)}, f32[24,768]{1,0:T(8,128)}, /...) custom-call(bf16[8,256,768]{2,1,0:T(8,128)(2,1)} %bitcast.47, ...), custom_call_target="tpu_custom_call", output_to_operand_aliasing={{10}: (19, {}), {8}: (20, {})} | custom-call | tf_op jit(solution)/shard_map/last/pallas_call | solution.py:1249
  405.8 0.8 slice.42
  406.6 0.6 dynamic-slice_bitcast_fusion
  407.2 0.8 slice_bitcast_fusion
  408.0 0.1 constant_dynamic-slice_fusion.2
  408.1 0.5 slice_bitcast_fusion.1
  408.7 0.6 fusion.5
  409.3 3.9 copy.56
  413.2 0.0 copy-done
  413.2 0.0 copy-start.5
  413.2 0.0 copy-start.2
  413.2 0.0 copy-start.1
  413.2 1.7 copy.57
  414.9 0.0 copy-done.4
  414.9 0.7 copy.58
  415.6 0.0 copy-done.6
  415.6 0.6 copy.59
  416.2 0.0 copy-done.3
  416.2 0.7 copy.60
  416.9 0.0 copy-done.5
  416.9 0.6 copy.61
  417.5 0.0 copy-done.2
  417.5 0.7 copy.62
  418.2 0.0 copy-done.1
  418.2 0.7 copy.63
  (12 shorter events, 0.1 us)
Async XLA Ops:
  409.3 3.9 copy-start
  413.2 1.7 copy-start.4
  413.2 2.4 copy-start.6
  413.2 3.0 copy-start.3
  413.2 3.7 copy-start.5
  413.2 4.3 %copy-start.2 = (f32[24,3072]{1,0:T(8,128)S(1)}, f32[24,3072]{1,0:T(8,128)}, u32[]{:S(2)}) copy-start(f32[24,3072]{1,0:T(8,128)} %get-tuple-element.127) | copy-start | bytes 884740
  413.2 5.0 %copy-start.1 = (f32[96,768]{1,0:T(8,128)S(1)}, f32[96,768]{1,0:T(8,128)}, u32[]{:S(2)}) copy-start(f32[96,768]{1,0:T(8,128)} %get-tuple-element.129) | copy-start | bytes 884740

commit v4 on v3

--- a/solution.py
+++ b/solution.py
@@ -1008,7 +1008,7 @@
 
 
 PANELS, BLOCKS, UNITS, SLOTS = 11, 8, 16, 6
-CHAINED = 12
+CHAINED = 8
 STEPS = PANELS + BLOCKS + UNITS - PANELS
 AFTER_STEP = {
     3: (0, 1, 2, 3),
@@ -1033,7 +1033,7 @@
     22: (14, 112, 500, 501, 407, 113, 506),
     23: (15, 211, 502, 503, 600, 601, 606, 114, 507, 308, 309, 212),
 }
-TAIL = (602, 310, 603, 504, 505, 607, 408, 409, 115, 213, 311, 604, 605, 508, 214, 509, 410, 312, 608, 609, 411, 215, 510, 313, 314, 511, 612, 315, 610, 611, 613, 614, 615)
+TAIL = (602, 310, 603, 504, 505, 607, 115, 213, 311, 604, 605, 214, 312, 608, 609, 215, 313, 314, 612, 315, 610, 611, 613, 614, 615)
 OUT_AT = (6, 9, 11, 13, 15, 17, 19, 21)
 
 

time: 419 us -> 421 us (level)
  no operation moved by 1% of the time
where the time goes in v4:
time: 421 us; the launch traced here: 420 us
  Pallas kernels  402 us (95%)
  local copies, waits for them, and re-layouts  15.8 us (4%)
    pallas_call x1, Pallas kernels, front(): pl.pallas_call(front_kernel, grid=(2 * blocks,), in_specs=[early(1, rows,...  242 us
    pallas_call x1, Pallas kernels, last(): pl.pallas_call(last_kernel, grid=(STEPS,), in_specs=[seq, pl.BlockSpec((r...  161 us
    unnamed x24, local copies, waits for them, and re-layouts  10.5 us

profile of v4, /device:TPU:0, one launch (start us, length us, event | category | flops | bytes accessed | tf_op | source)
XLA Modules:
  0.0 420.3 jit_solution(10131078994400032922)
XLA Ops:
  0.7 1.5 stack.49
  2.1 0.2 dynamic_update_slice.9
  2.3 0.8 dynamic_update_slice.11
  3.2 0.7 maximum_convert_fusion
  3.9 0.2 dynamic_update_slice.10
  4.1 0.6 fusion.4.vec_ref
  4.7 241.8 %front.1 = (bf16[2048,768]{1,0:T(8,128)(2,1)}, bf16[2048,2304]{1,0:T(8,128)(2,1)}, bf16[8,6,512,256]{3,2,1,0:T(8,128)(2,1)}, bf16[2048,768]{1,0:T(8,128)(2,1)}, ...) custom-call(bf16[8,256,768]{2,1,0:T(8,128)(2,1)} %bitcast.46, ...), custom_call_target="tpu_custom_call" | custom-call | tf_op jit(solution)/shard_map/front/pallas_call | solution.py:842
  246.5 160.6 %last.1 = (bf16[8,256,768]{2,1,0:T(8,128)(2,1)}, f32[24,2304]{1,0:T(8,128)}, f32[24,768]{1,0:T(8,128)}, f32[24,2304]{1,0:T(8,128)}, f32[24,768]{1,0:T(8,128)}, /...) custom-call(bf16[8,256,768]{2,1,0:T(8,128)(2,1)} %bitcast.47, ...), custom_call_target="tpu_custom_call", output_to_operand_aliasing={{10}: (19, {}), {8}: (20, {})} | custom-call | tf_op jit(solution)/shard_map/last/pallas_call | solution.py:1249
  407.1 0.8 slice.42
  407.9 0.6 dynamic-slice_bitcast_fusion
  408.5 0.8 slice_bitcast_fusion
  409.4 0.1 constant_dynamic-slice_fusion.2
  409.5 0.5 slice_bitcast_fusion.1
  410.0 0.6 fusion.5
  410.6 3.9 copy.56
  414.5 0.0 copy-done
  414.5 0.0 copy-start.5
  414.5 0.0 copy-start.2
  414.5 0.0 copy-start.1
  414.5 1.7 copy.57
  416.2 0.0 copy-done.4
  416.2 0.7 copy.58
  416.9 0.0 copy-done.6
  416.9 0.6 copy.59
  417.5 0.0 copy-done.3
  417.5 0.7 copy.60
  418.2 0.0 copy-done.5
  418.2 0.6 copy.61
  418.9 0.0 copy-done.2
  418.9 0.7 copy.62
  419.6 0.0 copy-done.1
  419.6 0.7 copy.63
  (12 shorter events, 0.1 us)
Async XLA Ops:
  410.6 3.9 copy-start
  414.5 1.7 copy-start.4
  414.5 2.4 copy-start.6
  414.5 3.0 copy-start.3
  414.5 3.7 copy-start.5
  414.5 4.3 %copy-start.2 = (f32[24,3072]{1,0:T(8,128)S(1)}, f32[24,3072]{1,0:T(8,128)}, u32[]{:S(2)}) copy-start(f32[24,3072]{1,0:T(8,128)} %get-tuple-element.127) | copy-start | bytes 884740
  414.5 5.0 %copy-start.1 = (f32[96,768]{1,0:T(8,128)S(1)}, f32[96,768]{1,0:T(8,128)}, u32[]{:S(2)}) copy-start(f32[96,768]{1,0:T(8,128)} %get-tuple-element.129) | copy-start | bytes 884740
